TPU v7x, 512 devices: a whole 4x8x8 slice. The times are simulated.
512 devices in a mesh: walker: 32 (over y_hi, z, core), chol: 16 (over y_lo, x).
Axes of the slice: x: 4, y: 8 (y_hi: 2, y_lo: 4; y = y_hi * 4 + y_lo), z: 8, core: 2. Of those that a mesh axis runs over, the one named last changes fastest.
Arguments:
- chol_vectors: bfloat16 [256, 768, 192], P('chol', 'walker'), may hold values from -0.2 to 0.2, as said below
- green: bfloat16 [64, 768, 192], P('walker'), may hold values from -6 to 6
Outputs:
- energy: float32 [64], P('walker')
- gradient: float32 [64, 768, 192], P('walker', 'chol')
Inputs may be any that keep to these rules, and one draw needn't show every extreme that they name: `chol_vectors`: independent entries of each vector; vector magnitudes differ from vector to vector.
All inputs are finite; a program needn't handle non-finite values.
Results may differ from a plain program's by a relative error of at most 0.0042.
Values may be sent and summed in bfloat16 or wider, within the bound.
No kernel may reach another device: no remote copies, remote signals or barrier semaphores. Data moves between devices by JAX's collectives and lax.ppermute only.
A program may use at most 64 MiB of HBM per device.

v0:
```python
import jax
import jax.numpy as jnp
from jax import lax
from jax.sharding import Mesh
from jax.sharding import PartitionSpec as P

NCHOL = 256
WALKER = ("walker_0", "walker_1", "walker_2")
CHOL = ("chol_0", "chol_1")


def laid_out(parts, dim):
    shape = list(parts.shape[1:])
    shape[dim] *= parts.shape[0]
    return jnp.moveaxis(parts, 0, dim).reshape(shape)


def gather_in_order(value, axes, turns):
    parts = value[None]
    for k in turns:
        parts = lax.all_gather(parts, axes[k], axis=0, tiled=True)
    current = [lax.axis_size(axes[k]) for k in reversed(turns)]
    parts = parts.reshape(*current, *value.shape)
    turned = sorted(range(len(turns)), key=lambda place: turns[len(turns) - 1 - place])
    return parts.transpose(*turned, *range(len(turns), parts.ndim)).reshape(-1, *value.shape)


def gathered_by_axis(value, axes, turns, dim):
    return laid_out(gather_in_order(value, axes, turns), dim)


def one_axis_at_a_time(value, axes):
    for axis in axes:
        value = lax.psum(value, axis)
    return value


def split_up(value, dim, devices):
    before, after = (value.shape[:dim], value.shape[dim + 1 :])
    return jnp.moveaxis(value.reshape(*before, devices, -1, *after), dim, 0)


def sum_at_owner(value, axis, dim):
    parts = split_up(value, dim, lax.axis_size(axis))
    arrived = lax.all_to_all(parts, axis, split_axis=0, concat_axis=0, tiled=True)
    return arrived.astype(jnp.float32).sum(axis=0)


def per_device(chol_vectors, green):
    width = green.shape[2]
    escale = 1.0 / (NCHOL * width)
    gscale = 1.0 / NCHOL**0.5
    whole = gathered_by_axis(chol_vectors, WALKER, (0, 1, 2), 1)
    tmat = jnp.einsum("kmi,wmj->wkij", whole, green, preferred_element_type=jnp.float32)
    partial_energy = jnp.sum(tmat * jnp.swapaxes(tmat, 2, 3), axis=(1, 2, 3)) * escale
    energy = one_axis_at_a_time(partial_energy, CHOL)
    tround = tmat.astype(jnp.bfloat16)
    terms = jnp.einsum("kmi,wkji->wmj", whole, tround, preferred_element_type=jnp.float32)
    gradient = sum_at_owner(terms.astype(jnp.bfloat16), CHOL, 1) * gscale
    return (energy, gradient)


def solution(mesh):
    torus = Mesh(
        mesh.devices.reshape(2, 8, 2, 4, 4),
        ("walker_0", "walker_1", "walker_2", "chol_0", "chol_1"),
    )
    placed = (P(CHOL, WALKER, None), P(WALKER, None, None))
    return jax.shard_map(
        per_device,
        mesh=torus,
        in_specs=placed,
        out_specs=(P(WALKER), P(WALKER, CHOL, None)),
        check_vma=False,
    )
```

profile of v0, /device:TPU:16, one launch (start us, length us, event | category | flops | bytes accessed | tf_op | source)
XLA Modules:
  0.0 175.1 jit_solution(13946936053803058149)
XLA Ops:
  7.2 0.0 copy-start
  7.2 0.0 all-gather.4.cloned.1.call-start
  7.2 14.4 %all-gather = bf16[32,24,192]{2,1,0:T(8,128)(2,1)} all-gather(bf16[16,24,192]{2,1,0:T(8,128)(2,1)} %param.2), channel_id=2, replica_groups=mesh['walker_0'=2,'walker_1'=8,'walker_2'=2,'chol_0'=4,'chol_1'=4] {'wal..., dimensions={0}, use_global_device_ids=true | all-gather | bytes 442368 | tf_op jit(solution)/shard_map/all_gather | solution.py:21
  21.6 0.0 all-gather.4.cloned.1.call-update
  21.6 0.0 all-gather.6.cloned.1.call-start
  21.7 54.5 %all-gather.4.cloned.1.call-done = bf16[16,16,24,192]{3,2,1,0:T(8,128)(2,1)} async-done(((bf16[2,16,24,192]{3,2,1,0:T(8,128)(2,1)}), bf16[16,16,24,192]{3,2,1,0:T(8,128)(2,1)}) %all-gather.4.cloned.1.call-update) | async-done | bytes 2359312 | tf_op jit(solution)/shard_map/all_gather | solution.py:21
  76.2 0.0 all-gather.6.cloned.1.call-update
  76.3 25.1 %all-gather.6.cloned.1.call-done = bf16[32,16,24,192]{3,2,1,0:T(8,128)(2,1)} async-done(((bf16[16,16,24,192]{3,2,1,0:T(8,128)(2,1)}), bf16[32,16,24,192]{3,2,1,0:T(8,128)(2,1)}) %all-gather.6.cloned.1.call-update) | async-done | bytes 4718608 | tf_op jit(solution)/shard_map/all_gather | solution.py:21
  101.3 3.5 %copy.11 = bf16[2,8,2,16,24,192]{5,4,2,1,0,3:T(8,128)(2,1)S(1)} copy(bf16[2,8,2,16,24,192]{5,4,3,0,1,2:T(8,128)(2,1)} %bitcast.54) | data formatting | bytes 9437184 | tf_op jit(solution)/shard_map/transpose | solution.py:25
  104.9 0.0 copy-start.1
  104.9 2.6 %copy-done.1 = bf16[2,8,2,16,24,192]{5,4,2,1,0,3:T(8,128)(2,1)} copy-done((bf16[2,8,2,16,24,192]{5,4,2,1,0,3:T(8,128)(2,1)}, bf16[2,8,2,16,24,192]{5,4,2,1,0,3:T(8,128)(2,1)S(1)}, u32[]{:S(2)}) %copy-start.1) | copy-done | bytes 4718616
  107.5 0.0 copy-done
  107.5 4.5 %fusion.5 = f32[2,192,16,192]{3,1,2,0:T(8,128)} fusion(bf16[16,768,192,1]{2,1,0,3:T(8,128)(2,1)S(1)} %bitcast.55, bf16[2,768,192]{1,2,0:T(8,128)(2,1)S(1)} %copy-done), kind=kOutput, calls=%fused_computation.8 | convolution fusion | flops 1811939328 | bytes 10027008 | tf_op jit(solution)/shard_map/kmi,wmj->wkij/dot_general | solution.py:54
  112.1 6.9 %copy.13 = f32[2,192,16,192]{1,3,2,0:T(8,128)} copy(f32[2,192,16,192]{3,1,2,0:T(8,128)} %fusion.5) | data formatting | bytes 9437184 | tf_op jit(solution)/shard_map/kmi,wmj->wkij/dot_general | solution.py:54
  118.9 7.2 %fusion.4 = bf16[2,768,192]{1,2,0:T(8,128)(2,1)S(1)} fusion(bf16[16,768,192,1]{2,1,0,3:T(8,128)(2,1)} %bitcast.56, f32[2,192,16,192]{1,3,2,0:T(8,128)} %copy.13), kind=kOutput, calls=%fused_computation.7 | convolution fusion | flops 1811939328 | bytes 10027008 | tf_op jit(solution)/shard_map/kmi,wkji->wmj/dot_general | solution.py:58
  126.2 0.3 copy.15
  126.4 1.0 copy.16
  127.4 7.6 %all-to-all-start = ((bf16[16,2,48,192]{3,2,1,0:T(8,128)(2,1)}), bf16[16,2,48,192]{3,2,1,0:T(8,128)(2,1)S(1)}, u32[]{:S(2)}, u32[]{:S(2)}) async-start(bf16[16,2,48,192]{3,2,1,0:T(8,128)(2,1)} %copy.16), calls=%async_computation | async-start | bytes 1572864 | tf_op jit(solution)/shard_map/all_to_all | solution.py:45
  135.0 5.6 %fusion = f32[2]{0:T(128)S(1)} fusion(f32[2,192,16,192]{3,1,2,0:T(8,128)} %fusion.5, f32[2,192,16,192]{1,3,2,0:T(8,128)} %copy.13), kind=kLoop, calls=%fused_computation.1 | loop fusion | flops 2359294 | bytes 9437192 | tf_op jit(solution)/shard_map/reduce_sum | solution.py:55
  140.7 15.9 %psum.14 = f32[2]{0:T(128)S(1)} all-reduce(f32[2]{0:T(128)S(1)} %broadcast_multiply_fusion.1), channel_id=1, replica_groups=mesh['walker_0'=2,'walker_1'=8,'walker_2'=2,'chol_0'=4,'chol_1'=4] {'cho..., use_global_device_ids=true, to_apply=%region_1.0 | all-reduce | flops 2 | bytes 16 | tf_op jit(solution)/shard_map/psum | solution.py:34
  156.6 10.9 %psum.15 = f32[2]{0:T(128)} all-reduce(f32[2]{0:T(128)S(1)} %psum.14), channel_id=1, replica_groups=mesh['walker_0'=2,'walker_1'=8,'walker_2'=2,'chol_0'=4,'chol_1'=4] {'cho..., use_global_device_ids=true, to_apply=%region_2.0 | all-reduce | flops 2 | bytes 16 | tf_op jit(solution)/shard_map/psum | solution.py:34
  167.5 0.0 all-to-all-done
  167.5 0.1 convert_reduce_fusion
  167.6 0.6 broadcast_multiply_fusion
  (1 shorter events, 0.0 us)
Async XLA Ops:
  7.2 100.3 %copy-start = (bf16[2,768,192]{1,2,0:T(8,128)(2,1)S(1)}, bf16[2,768,192]{1,2,0:T(8,128)(2,1)}, u32[]{:S(2)}) copy-start(bf16[2,768,192]{1,2,0:T(8,128)(2,1)} %param.3) | copy-start | bytes 1769476
  7.2 69.1 %all-gather.4.cloned.1.call-start = ((), (), s32[]{:S(2)}) async-start(), calls=%async_computation.1 | async-start | bytes 3538944 | tf_op jit(solution)/shard_map/all_gather | solution.py:21
  21.6 79.7 %all-gather.6.cloned.1.call-start = ((), (), s32[]{:S(2)}) async-start(), calls=%async_computation.2 | async-start | bytes 9437184 | tf_op jit(solution)/shard_map/all_gather | solution.py:21
  104.9 2.6 %copy-start.1 = (bf16[2,8,2,16,24,192]{5,4,2,1,0,3:T(8,128)(2,1)}, bf16[2,8,2,16,24,192]{5,4,2,1,0,3:T(8,128)(2,1)S(1)}, u32[]{:S(2)}) copy-start(bf16[2,8,2,16,24,192]{5,4,2,1,0,3:T(8,128)(2,1)S(1)} %copy.11) | copy-start | bytes 14155780
  127.4 40.0 %all-to-all-start = ((bf16[16,2,48,192]{3,2,1,0:T(8,128)(2,1)}), bf16[16,2,48,192]{3,2,1,0:T(8,128)(2,1)S(1)}, u32[]{:S(2)}, u32[]{:S(2)}) async-start(bf16[16,2,48,192]{3,2,1,0:T(8,128)(2,1)} %copy.16), calls=%async_computation | async-start | bytes 1572864 | tf_op jit(solution)/shard_map/all_to_all | solution.py:45
Sparse Core Ops, SparseCore 0:
  21.8 54.4 all-gather.3
  78.3 22.9 all-gather.5
where the time goes:
time: 176 us; the launch traced here: 175 us
  waiting for transfers between devices  79.6 us (45%)
  blocking collectives  41.2 us (23%)
  local copies, waits for them, and re-layouts  14.3 us (8%)
  between operations  14.1 us (8%)
  matrix products  11.8 us (7%)
  starting transfers between devices  7.63 us (4%)
  other arithmetic  6.44 us (4%)
    all_gather x2, waiting for transfers between devices, gather_in_order(): parts = lax.all_gather(parts, axes[k], axis=0, tiled=True)  79.6 us
    psum x2, blocking collectives, one_axis_at_a_time(): value = lax.psum(value, axis)  26.8 us
    all_gather x1, blocking collectives, gather_in_order(): parts = lax.all_gather(parts, axes[k], axis=0, tiled=True)  14.4 us
    all_to_all x1, starting transfers between devices, sum_at_owner(): lax.all_to_all(parts, axis, split_axis=0, concat_axis=0, tiled=True)  7.55 us
    dot_general x1, matrix products, per_device(): jnp.einsum('kmi,wkji->wmj', whole, tround, preferred_element_type=jnp.flo...  7.24 us
    dot_general x1, local copies, waits for them, and re-layouts, per_device(): jnp.einsum('kmi,wmj->wkij', whole, green, preferred_element_type=jnp.floa...  6.87 us
    reduce_sum x1, other arithmetic, per_device(): jnp.sum(tmat * jnp.swapaxes(tmat, 2, 3), axis=(1, 2, 3)) * escale  5.65 us
    dot_general x1, matrix products, per_device(): jnp.einsum('kmi,wmj->wkij', whole, green, preferred_element_type=jnp.floa...  4.55 us
  transfers between devices with their start and end apart: 3, of which 2 were waited for; matrix products, arithmetic and copies ran while one was open for 3% of the time, Pallas kernels for 0%

commit v1 on v0

v1 whole, which is shorter than its diff:
```python
import jax
import jax.numpy as jnp
from jax import lax
from jax.experimental import pallas as pl
from jax.experimental.pallas import tpu as pltpu
from jax.sharding import Mesh
from jax.sharding import PartitionSpec as P

M = 768
NOCC = 192
NCHOL = 256
WALKER = ("y_hi", "z", "core")
CHOL = ("y_lo", "x")
PLACES = 16
KVEC = 16
ROWS = 24
WPER = 2
WIDE = KVEC * NOCC
CHUNK = 4 * NOCC
PAY = 160
VMEM_LIMIT = 56 * 1024 * 1024


def whole(shape=None):
    return pl.BlockSpec(memory_space=pltpu.VMEM)


def pack_kernel(chol_ref, out_ref):
    for k in range(0, KVEC, 2):
        pair = jnp.concatenate([chol_ref[k], chol_ref[k + 1]], axis=1)
        out_ref[:, k * NOCC : (k + 2) * NOCC] = pair


def pack(chol):
    return pl.pallas_call(
        pack_kernel,
        out_shape=jax.ShapeDtypeStruct((ROWS, WIDE), jnp.bfloat16),
        in_specs=[whole()],
        out_specs=whole(),
        name="pack",
    )(chol)


def split3(value):
    high = value.astype(jnp.bfloat16).astype(jnp.float32)
    left = value - high
    mid = left.astype(jnp.bfloat16).astype(jnp.float32)
    return high, mid, left - mid


def work_kernel(turn_ref, gt_ref, g_ref, own_ref, sib_ref, pay_ref, stack):
    half = PLACES * ROWS
    xs = (own_ref, sib_ref)
    for c in range(0, WIDE, CHUNK):
        part = jnp.dot(gt_ref[:, :half], own_ref[:, c : c + CHUNK], preferred_element_type=jnp.float32)
        part = part + jnp.dot(gt_ref[:, half:], sib_ref[:, c : c + CHUNK], preferred_element_type=jnp.float32)
        for q in range(CHUNK // NOCC):
            for w in range(WPER):
                tile = part[w * NOCC : (w + 1) * NOCC, q * NOCC : (q + 1) * NOCC]
                stack[w, c + q * NOCC : c + (q + 1) * NOCC, :] = tile.astype(jnp.bfloat16)
    straight = turn_ref[0] == 0
    terms = []
    energy = []
    for w in range(WPER):
        both = [jnp.dot(x[...], stack[w], preferred_element_type=jnp.float32) for x in xs]
        total = jnp.zeros((8, NOCC), jnp.float32)
        for s in range(2):
            green = g_ref[w, s * half : (s + 1) * half, :].astype(jnp.float32)
            total = total + (both[s] * green).reshape(half // 8, 8, NOCC).sum(axis=0)
        energy.append(jnp.sum(total))
        terms.append((jnp.where(straight, both[0], both[1]), jnp.where(straight, both[1], both[0])))
    row = lax.broadcasted_iota(jnp.int32, (16, 128), 0)
    carried = jnp.zeros((16, 128), jnp.float32)
    for w in range(WPER):
        filled = jnp.full((16, 128), energy[w], jnp.float32)
        for n, value in enumerate(split3(filled)):
            carried = jnp.where(row == 8 * w + n, value, carried)
    carried = carried.astype(jnp.bfloat16)
    for z in range(8):
        for y in range(2):
            block = z * 2 + y
            place = y * 8 + z
            here = [
                jnp.concatenate([low[block * ROWS : (block + 1) * ROWS], high[block * ROWS : (block + 1) * ROWS]], axis=0)
                for low, high in terms
            ]
            pay_ref[place, 0:48, :] = here[0][:, :128].astype(jnp.bfloat16)
            pay_ref[place, 48:96, :] = here[1][:, :128].astype(jnp.bfloat16)
            rest = jnp.concatenate([here[0][:, 128:], here[1][:, 128:]], axis=1)
            pay_ref[place, 96:144, :] = rest.astype(jnp.bfloat16)
            pay_ref[place, 144:160, :] = carried


def work(turn, gt, g, own, sib):
    return pl.pallas_call(
        work_kernel,
        out_shape=jax.ShapeDtypeStruct((PLACES, PAY, 128), jnp.bfloat16),
        in_specs=[pl.BlockSpec(memory_space=pltpu.SMEM)] + [whole()] * 4,
        out_specs=whole(),
        scratch_shapes=[pltpu.VMEM((WPER, WIDE, NOCC), jnp.bfloat16)],
        compiler_params=pltpu.CompilerParams(vmem_limit_bytes=VMEM_LIMIT),
        name="work",
    )(turn, gt, g, own, sib)


def close_kernel(got_ref, energy_ref, gradient_ref):
    escale = 1.0 / (NCHOL * NOCC)
    gscale = 1.0 / NCHOL**0.5
    total = got_ref[0].astype(jnp.float32)
    for n in range(1, PLACES):
        total = total + got_ref[n].astype(jnp.float32)
    for w in range(WPER):
        rest = total[96:144, 64 * w : 64 * (w + 1)]
        gradient_ref[w] = jnp.concatenate([total[48 * w : 48 * (w + 1)], rest], axis=1) * gscale
        base = 144 + 8 * w
        parts = total[base : base + 1] + total[base + 1 : base + 2] + total[base + 2 : base + 3]
        energy_ref[w] = parts[0, 0] * escale


def close(got):
    return pl.pallas_call(
        close_kernel,
        out_shape=(
            jax.ShapeDtypeStruct((WPER,), jnp.float32),
            jax.ShapeDtypeStruct((WPER, 48, NOCC), jnp.float32),
        ),
        in_specs=[whole()],
        out_specs=(pl.BlockSpec(memory_space=pltpu.SMEM), whole()),
        name="close",
    )(got)


def pairs(axis):
    return [(0, 1), (1, 0)]


def per_device(chol_vectors, green):
    y_hi = lax.axis_index("y_hi")
    core = lax.axis_index("core")
    packed = pack(chol_vectors)
    other = lax.ppermute(packed, "y_hi", pairs("y_hi"))
    first = jnp.where(y_hi == 0, packed, other)
    second = jnp.where(y_hi == 0, other, packed)
    mine = lax.all_gather(jnp.concatenate([first, second], axis=0), "z", axis=0, tiled=True)
    theirs = lax.ppermute(mine, "core", pairs("core"))
    split = green.reshape(WPER, 2, 8, 2, ROWS, NOCC)
    split = jnp.where(core == 0, split, jnp.flip(split, axis=3))
    g = split.transpose(0, 3, 2, 1, 4, 5).reshape(WPER, M, NOCC)
    gt = split.transpose(0, 5, 3, 2, 1, 4).reshape(WPER * NOCC, M)
    payload = work(core.reshape(1), gt, g, mine, theirs)
    got = lax.all_to_all(payload, CHOL, split_axis=0, concat_axis=0, tiled=True)
    return close(got)


def solution(mesh):
    torus = Mesh(
        mesh.devices.reshape(2, 8, 2, 4, 4),
        ("y_hi", "z", "core", "y_lo", "x"),
    )
    return jax.shard_map(
        per_device,
        mesh=torus,
        in_specs=(P(CHOL, WALKER, None), P(WALKER, None, None)),
        out_specs=(P(WALKER), P(WALKER, CHOL, None)),
        check_vma=False,
    )
```

time: 176 us -> 130 us (0.74)
  the two profiles are of different devices: /device:TPU:16 before, /device:TPU:1 now
where the time goes in v1:
time: 130 us
  waiting for transfers between devices  54 us (42%)
  blocking collectives  25.3 us (19%)
  starting transfers between devices  14.1 us (11%)
  between operations  14.1 us (11%)
  Pallas kernels  12.4 us (10%)
  local copies, waits for them, and re-layouts  7.87 us (6%)
  other arithmetic  1.93 us (1%)
    all_gather x1, waiting for transfers between devices, per_device(): lax.all_gather(jnp.concatenate([first, second], axis=0), 'z', axis=0, til...  48.1 us
    all_to_all x1, blocking collectives, per_device(): got = lax.all_to_all(payload, CHOL, split_axis=0, concat_axis=0, tiled=True)  25.3 us
    pallas_call x1, Pallas kernels, work(): pl.pallas_call(work_kernel, out_shape=jax.ShapeDtypeStruct((PLACES, PAY,...  8.9 us
    ppermute x1, starting transfers between devices, per_device(): other = lax.ppermute(packed, 'y_hi', pairs('y_hi'))  8.27 us
    ppermute x1, waiting for transfers between devices, per_device(): other = lax.ppermute(packed, 'y_hi', pairs('y_hi'))  5.88 us
    ppermute x1, starting transfers between devices, per_device(): theirs = lax.ppermute(mine, 'core', pairs('core'))  5.78 us
    reshape x2, local copies, waits for them, and re-layouts, per_device(): gt = split.transpose(0, 5, 3, 2, 1, 4).reshape(WPER * NOCC, M)  3.36 us
    unnamed x3, local copies, waits for them, and re-layouts  2.74 us
  transfers between devices with their start and end apart: 3, of which 2 were waited for; matrix products, arithmetic and copies ran while one was open for 5% of the time, Pallas kernels for 0%

profile of v1, /device:TPU:1, one launch (start us, length us, event | category | flops | bytes accessed | tf_op | source)
XLA Modules:
  0.0 129.7 jit_solution(6160812710946369442)
XLA Ops:
  7.2 0.0 all-gather.2.cloned.1.call-start
  7.2 1.7 %pack.1 = bf16[24,3072]{1,0:T(8,128)(2,1)} custom-call(bf16[16,24,192]{2,1,0:T(8,128)(2,1)} %chol_ref.1), custom_call_target="tpu_custom_call" | custom-call | tf_op jit(solution)/shard_map/pack/pallas_call | solution.py:35
  8.9 8.3 %collective-permute-start = (bf16[24,3072]{1,0:T(8,128)(2,1)}, bf16[24,3072]{1,0:T(8,128)(2,1)S(1)}, u32[]{:S(2)}, u32[]{:S(2)}) collective-permute-start(bf16[24,3072]{1,0:T(8,128)(2,1)} %pack.1), channel_id=1, source_target_pairs={{0,256},{256,0},{1,257},{257,1},{2,258},{258,2},{3,259},{259,3},{4... | collective-permute-start | bytes 442376 | tf_op jit(solution)/shard_map/ppermute | solution.py:141
  17.2 5.9 %collective-permute-done = bf16[24,3072]{1,0:T(8,128)(2,1)S(1)} collective-permute-done((bf16[24,3072]{1,0:T(8,128)(2,1)}, bf16[24,3072]{1,0:T(8,128)(2,1)S(1)}, u32[]{:S(2)}, u32[]{:S(2)}) %collective-permute-start) | collective-permute-done | bytes 147488 | tf_op jit(solution)/shard_map/ppermute | solution.py:141
  23.1 0.9 broadcast_select_fusion.1
  24.0 0.7 pad_maximum_fusion
  24.7 0.0 all-gather.2.cloned.1.call-update
  24.7 48.1 %all-gather.2.cloned.1.call-done.own_ref = bf16[384,3072]{1,0:T(8,128)(2,1)} async-done(((bf16[48,3072]{1,0:T(8,128)(2,1)}), bf16[384,3072]{1,0:T(8,128)(2,1)}) %all-gather.2.cloned.1.call-update) | async-done | bytes 2359312 | tf_op jit(solution)/shard_map/all_gather | solution.py:144
  72.9 5.8 %collective-permute-start.1 = (bf16[384,3072]{1,0:T(8,128)(2,1)}, bf16[384,3072]{1,0:T(8,128)(2,1)S(1)}, u32[]{:S(2)}, u32[]{:S(2)}) collective-permute-start(bf16[384,3072]{1,0:T(8,128)(2,1)} %all-gather.2.cloned.1.call-done.own_ref), channel_id=1, source_target_pairs={{0,16},{16,0},{1,17},{17,1},{2,18},{18,2},{3,19},{19,3},{4,20},{20... | collective-permute-start | bytes 7077896 | tf_op jit(solution)/shard_map/ppermute | solution.py:145
  78.7 1.3 %copy.7 = bf16[2,768,192]{2,1,0:T(8,128)(2,1)S(1)} copy(bf16[2,768,192]{1,2,0:T(8,128)(2,1)} %param.3) | data formatting | bytes 1179648 | tf_op args[1]
  80.0 0.3 fusion
  80.3 1.0 copy.9
  81.2 0.8 copy.8
  82.0 1.2 reshape.18
  83.3 2.1 %copy.10.gt_ref = bf16[384,768]{1,0:T(8,128)(2,1)} copy(bf16[384,768]{0,1:T(8,128)(2,1)} %reshape.18) | data formatting | bytes 1179648 | tf_op jit(solution)/shard_map/reshape | solution.py:149
  85.4 0.0 collective-permute-done.1.sib_ref
  85.4 0.0 copy-start
  85.4 1.4 %copy-done = bf16[384,3072]{1,0:T(8,128)(2,1)} copy-done((bf16[384,3072]{1,0:T(8,128)(2,1)}, bf16[384,3072]{1,0:T(8,128)(2,1)S(1)}, u32[]{:S(2)}) %copy-start) | copy-done | bytes 2359320
  86.8 8.9 %work.1 = bf16[16,160,128]{2,1,0:T(8,128)(2,1)} custom-call(s32[1]{0:T(128)} %bitcast.turn_ref, bf16[384,768]{1,0:T(8,128)(2,1)} %copy.10.gt_ref, bf16[2,768,192]{2,1,0:T(8,128)(2,1)} %bitcast.10, bf16[384,3072]{1,0:T(8,128)(2,1)} %all-gather.2.cloned.1.call-done.own_ref, bf16[384,3072]{1,0:T(8,128)(2,1)} %copy-done), custom_call_target="tpu_custom_call" | custom-call | tf_op jit(solution)/shard_map/work/pallas_call | solution.py:95
  95.7 25.3 %all_to_all.5.got_ref = bf16[16,160,128]{2,1,0:T(8,128)(2,1)} all-to-all(bf16[16,160,128]{2,1,0:T(8,128)(2,1)} %work.1), channel_id=1, replica_groups=mesh['y_hi'=2,'z'=8,'core'=2,'y_lo'=4,'x'=4] {'y_lo','x'}, dimensions={0} | all-to-all | bytes 1310720 | tf_op jit(solution)/shard_map/all_to_all | solution.py:151
  121.0 1.8 %close.1 = (f32[2]{0:T(128)}, f32[2,48,192]{2,1,0:T(8,128)}) custom-call(bf16[16,160,128]{2,1,0:T(8,128)(2,1)} %all_to_all.5.got_ref), custom_call_target="tpu_custom_call" | custom-call | tf_op jit(solution)/shard_map/close/pallas_call | solution.py:121
Async XLA Ops:
  7.2 65.7 %all-gather.2.cloned.1.call-start = ((), (), s32[]{:S(2)}) async-start(), calls=%async_computation.1 | async-start | bytes 2654208 | tf_op jit(solution)/shard_map/all_gather | solution.py:144
  8.9 14.2 %collective-permute-start = (bf16[24,3072]{1,0:T(8,128)(2,1)}, bf16[24,3072]{1,0:T(8,128)(2,1)S(1)}, u32[]{:S(2)}, u32[]{:S(2)}) collective-permute-start(bf16[24,3072]{1,0:T(8,128)(2,1)} %pack.1), channel_id=1, source_target_pairs={{0,256},{256,0},{1,257},{257,1},{2,258},{258,2},{3,259},{259,3},{4... | collective-permute-start | bytes 442376 | tf_op jit(solution)/shard_map/ppermute | solution.py:141
  72.9 12.6 %collective-permute-start.1 = (bf16[384,3072]{1,0:T(8,128)(2,1)}, bf16[384,3072]{1,0:T(8,128)(2,1)S(1)}, u32[]{:S(2)}, u32[]{:S(2)}) collective-permute-start(bf16[384,3072]{1,0:T(8,128)(2,1)} %all-gather.2.cloned.1.call-done.own_ref), channel_id=1, source_target_pairs={{0,16},{16,0},{1,17},{17,1},{2,18},{18,2},{3,19},{19,3},{4,20},{20... | collective-permute-start | bytes 7077896 | tf_op jit(solution)/shard_map/ppermute | solution.py:145
  85.4 1.4 %copy-start = (bf16[384,3072]{1,0:T(8,128)(2,1)}, bf16[384,3072]{1,0:T(8,128)(2,1)S(1)}, u32[]{:S(2)}) copy-start(bf16[384,3072]{1,0:T(8,128)(2,1)S(1)} %collective-permute-done.1.sib_ref) | copy-start | bytes 7077892
Sparse Core Ops, SparseCore 0:
  24.9 47.9 all-gather.1

commit v2 on v1

v2 whole, which is shorter than its diff:
```python
import jax
import jax.numpy as jnp
from jax import lax
from jax.experimental import pallas as pl
from jax.experimental.pallas import tpu as pltpu
from jax.sharding import Mesh
from jax.sharding import PartitionSpec as P

M = 768
NOCC = 192
NCHOL = 256
WALKER = ("y_hi", "z", "core")
CHOL = ("y_lo", "x")
ROWS = 24
BLOCK = 2 * ROWS
WPER = 2
QUARTER = 4
CHUNK = QUARTER * NOCC
DATA = 3 * BLOCK
CARRY = 16
VMEM_LIMIT = 40 * 1024 * 1024


def whole():
    return pl.BlockSpec(memory_space=pltpu.VMEM)


def pack_kernel(chol_ref, out_ref):
    for q in range(4):
        for k in range(0, QUARTER, 2):
            first = q * QUARTER + k
            pair = jnp.concatenate([chol_ref[first], chol_ref[first + 1]], axis=1)
            out_ref[q, :, k * NOCC : (k + 2) * NOCC] = pair


def pack(chol):
    return pl.pallas_call(
        pack_kernel,
        out_shape=jax.ShapeDtypeStruct((4, ROWS, CHUNK), jnp.bfloat16),
        in_specs=[whole()],
        out_specs=whole(),
        name="pack",
    )(chol)


def split3(value):
    high = value.astype(jnp.bfloat16).astype(jnp.float32)
    left = value - high
    mid = left.astype(jnp.bfloat16).astype(jnp.float32)
    return high, mid, left - mid


def carry(values):
    row = lax.broadcasted_iota(jnp.int32, (CARRY, 128), 0)
    out = jnp.zeros((CARRY, 128), jnp.float32)
    for n, value in enumerate(values):
        filled = jnp.broadcast_to(value, (CARRY, 128))
        for p, part in enumerate(split3(filled)):
            out = jnp.where(row == 3 * n + p, part, out)
    return out.astype(jnp.bfloat16)


def carried(rows, n):
    return rows[3 * n : 3 * n + 1] + rows[3 * n + 1 : 3 * n + 2] + rows[3 * n + 2 : 3 * n + 3]


def work_kernel(mine_ref, theirs_ref, own_ref, sib_ref, pay_ref, stack):
    side = lax.axis_index("y_hi")
    chunks = (own_ref, sib_ref)
    half = M // 2
    greens = (mine_ref, theirs_ref)
    for c, x_ref in enumerate(chunks):
        for g, green in enumerate(greens):
            part = jnp.dot(green[:, :half], x_ref[:, 0].reshape(half, CHUNK), preferred_element_type=jnp.float32)
            part = part + jnp.dot(green[:, half:], x_ref[:, 1].reshape(half, CHUNK), preferred_element_type=jnp.float32)
            for q in range(QUARTER):
                for w in range(WPER):
                    tile = part[w * NOCC : (w + 1) * NOCC, q * NOCC : (q + 1) * NOCC]
                    stack[c, g * WPER + w, q * NOCC : (q + 1) * NOCC, :] = tile.astype(jnp.bfloat16)
    diagonal = lax.broadcasted_iota(jnp.int32, (NOCC, NOCC), 0) == lax.broadcasted_iota(jnp.int32, (NOCC, NOCC), 1)
    energies = []
    for g, green in enumerate(greens):
        y = side if g == 0 else 1 - side
        traces = [jnp.zeros((NOCC, NOCC), jnp.float32) for _ in range(WPER)]
        for m in range(2):
            grads = []
            for w in range(WPER):
                n = g * WPER + w
                grad = jnp.dot(own_ref[:, m].reshape(half, CHUNK), stack[0, n], preferred_element_type=jnp.float32)
                grad = grad + jnp.dot(sib_ref[:, m].reshape(half, CHUNK), stack[1, n], preferred_element_type=jnp.float32)
                rounded = grad.astype(jnp.bfloat16)
                traces[w] = traces[w] + jnp.dot(
                    green[w * NOCC : (w + 1) * NOCC, m * half : (m + 1) * half], rounded, preferred_element_type=jnp.float32
                )
                grads.append(grad)
            rest = jnp.concatenate([grads[0][:, 128:], grads[1][:, 128:]], axis=1).astype(jnp.bfloat16)
            first, second = (grad[:, :128].astype(jnp.bfloat16) for grad in grads)
            for b in range(8):
                place = m * 8 + b
                x, y_lo = place % 4, place // 4
                base = y_lo * DATA
                rows = slice(b * BLOCK, (b + 1) * BLOCK)
                pay_ref[x, y, base : base + BLOCK, :] = first[rows]
                pay_ref[x, y, base + BLOCK : base + 2 * BLOCK, :] = second[rows]
                pay_ref[x, y, base + 2 * BLOCK : base + DATA, :] = rest[rows]
        energies = [jnp.sum(jnp.where(diagonal, trace, 0.0)) for trace in traces]
        rows = carry(energies)
        for x in range(4):
            pay_ref[x, y, 4 * DATA : 4 * DATA + CARRY, :] = rows


def work(mine, theirs, own, sib):
    return pl.pallas_call(
        work_kernel,
        out_shape=jax.ShapeDtypeStruct((4, 2, 4 * DATA + CARRY, 128), jnp.bfloat16),
        in_specs=[whole()] * 4,
        out_specs=whole(),
        scratch_shapes=[pltpu.VMEM((2, 2 * WPER, CHUNK, NOCC), jnp.bfloat16)],
        compiler_params=pltpu.CompilerParams(vmem_limit_bytes=VMEM_LIMIT),
        name="work",
    )(mine, theirs, own, sib)


def middle_kernel(got_ref, pay_ref):
    for y in range(2):
        total = got_ref[0, y].astype(jnp.float32)
        for x in range(1, 4):
            total = total + got_ref[x, y].astype(jnp.float32)
        rows = carry([carried(total[4 * DATA :], w)[:, :1] for w in range(WPER)])
        for y_lo in range(4):
            pay_ref[y * 4 + y_lo, :DATA, :] = total[y_lo * DATA : (y_lo + 1) * DATA].astype(jnp.bfloat16)
            pay_ref[y * 4 + y_lo, DATA:, :] = rows


def middle(got):
    return pl.pallas_call(
        middle_kernel,
        out_shape=jax.ShapeDtypeStruct((8, DATA + CARRY, 128), jnp.bfloat16),
        in_specs=[whole()],
        out_specs=whole(),
        name="middle",
    )(got)


def close_kernel(got_ref, energy_ref, gradient_ref):
    escale = 1.0 / (NCHOL * NOCC)
    gscale = 1.0 / NCHOL**0.5
    total = got_ref[0].astype(jnp.float32)
    for n in range(1, 8):
        total = total + got_ref[n].astype(jnp.float32)
    for w in range(WPER):
        rest = total[2 * BLOCK : DATA, 64 * w : 64 * (w + 1)]
        gradient_ref[w] = jnp.concatenate([total[BLOCK * w : BLOCK * (w + 1)], rest], axis=1) * gscale
        energy_ref[w] = carried(total[DATA:], w)[0, 0] * escale


def close(got):
    return pl.pallas_call(
        close_kernel,
        out_shape=(
            jax.ShapeDtypeStruct((WPER,), jnp.float32),
            jax.ShapeDtypeStruct((WPER, BLOCK, NOCC), jnp.float32),
        ),
        in_specs=[whole()],
        out_specs=(pl.BlockSpec(memory_space=pltpu.SMEM), whole()),
        name="close",
    )(got)


def swap(value, axis):
    return lax.ppermute(value, axis, [(0, 1), (1, 0)])


def exchange(value, axes):
    return lax.all_to_all(value, axes, split_axis=0, concat_axis=0, tiled=True)


def per_device(chol_vectors, green):
    packed = exchange(pack(chol_vectors), ("y_hi", "core"))
    turned = jnp.swapaxes(green, 1, 2).reshape(WPER * NOCC, M)
    packed, turned = lax.optimization_barrier((packed, turned))
    other = swap(turned, "y_hi")
    block = packed.reshape(2, BLOCK, CHUNK)
    own = exchange(jnp.broadcast_to(block[None], (8, *block.shape)), "z")
    own, other = lax.optimization_barrier((own, other))
    sib = swap(own, "core")
    payload = work(turned, other, own.reshape(8, 2, BLOCK, CHUNK), sib.reshape(8, 2, BLOCK, CHUNK))
    got = exchange(middle(exchange(payload, "x")), ("y_hi", "y_lo"))
    return close(got)


def solution(mesh):
    torus = Mesh(
        mesh.devices.reshape(2, 8, 2, 4, 4),
        ("y_hi", "z", "core", "y_lo", "x"),
    )
    return jax.shard_map(
        per_device,
        mesh=torus,
        in_specs=(P(CHOL, WALKER, None), P(WALKER, None, None)),
        out_specs=(P(WALKER), P(WALKER, CHOL, None)),
        check_vma=False,
    )
```

time: 130 us -> 116 us (0.89); the launches traced: 130 us -> 114 us
  blocking collectives: 25.3 us -> 53.7 us
  waiting for transfers between devices: 54 us -> 32.5 us
  between operations: 14.1 us -> 0.66 us
  local copies, waits for them, and re-layouts: 7.87 us -> 1.1 us
  other arithmetic: 1.93 us -> 0 us
    all_gather x1 -> x0, waiting for transfers between devices: 48.1 us -> none  [per_device(): lax.all_gather(jnp.concatenate([first, second], axis=0), 'z', axis=0, til...]
    all_to_all x1 -> x3, blocking collectives: 25.3 us -> 53.7 us  [exchange(): return lax.all_to_all(value, axes, split_axis=0, concat_axis=0, tiled=True)]
    ppermute x2, waiting for transfers between devices: 5.88 us -> 25.8 us  [swap(): return lax.ppermute(value, axis, [(0, 1), (1, 0)])]
    ppermute x2, starting transfers between devices: 14.1 us -> 4.54 us  [swap(): return lax.ppermute(value, axis, [(0, 1), (1, 0)])]
    all_to_all x0 -> x1, starting transfers between devices: none -> 8.59 us  [exchange(): return lax.all_to_all(value, axes, split_axis=0, concat_axis=0, tiled=True)]
    all_to_all x0 -> x1, waiting for transfers between devices: none -> 6.66 us  [exchange(): return lax.all_to_all(value, axes, split_axis=0, concat_axis=0, tiled=True)]
    reshape x2 -> x0, local copies, waits for them, and re-layouts: 3.36 us -> none  [per_device(): gt = split.transpose(0, 5, 3, 2, 1, 4).reshape(WPER * NOCC, M)]
    unnamed x3 -> x2, local copies, waits for them, and re-layouts: 2.74 us -> 0.01 us
  transfers between devices with their start and end apart: 3 -> 3, of which waited for: 2 -> 3; matrix products, arithmetic and copies ran while one was open for 5% -> 0% of each run, Pallas kernels for 0% -> 0%
where the time goes in v2:
time: 116 us; the launch traced here: 114 us
  blocking collectives  53.7 us (46%)
  waiting for transfers between devices  32.5 us (28%)
  Pallas kernels  13.2 us (11%)
  starting transfers between devices  13.1 us (11%)
    all_to_all x3, blocking collectives, exchange(): return lax.all_to_all(value, axes, split_axis=0, concat_axis=0, tiled=True)  53.7 us
    ppermute x2, waiting for transfers between devices, swap(): return lax.ppermute(value, axis, [(0, 1), (1, 0)])  25.8 us
    all_to_all x1, starting transfers between devices, exchange(): return lax.all_to_all(value, axes, split_axis=0, concat_axis=0, tiled=True)  8.59 us
    pallas_call x1, Pallas kernels, work(): pl.pallas_call(work_kernel, out_shape=jax.ShapeDtypeStruct((4, 2, 4 * DAT...  7.55 us
    all_to_all x1, waiting for transfers between devices, exchange(): return lax.all_to_all(value, axes, split_axis=0, concat_axis=0, tiled=True)  6.66 us
    ppermute x2, starting transfers between devices, swap(): return lax.ppermute(value, axis, [(0, 1), (1, 0)])  4.54 us
  transfers between devices with their start and end apart: 3, of which 3 were waited for; matrix products, arithmetic and copies ran while one was open for 0% of the time, Pallas kernels for 0%

profile of v2, /device:TPU:1, one launch (start us, length us, event | category | flops | bytes accessed | tf_op | source)
XLA Modules:
  0.0 114.3 jit_solution(15796450523764464574)
XLA Ops:
  0.6 1.7 %pack.1 = bf16[4,24,768]{2,1,0:T(8,128)(2,1)} custom-call(bf16[16,24,192]{2,1,0:T(8,128)(2,1)} %chol_ref.1), custom_call_target="tpu_custom_call" | custom-call | tf_op jit(solution)/shard_map/pack/pallas_call | solution.py:37
  2.3 18.4 %all_to_all.20 = bf16[4,24,768]{2,1,0:T(8,128)(2,1)S(1)} all-to-all(bf16[4,24,768]{2,1,0:T(8,128)(2,1)} %pack.1), channel_id=1, replica_groups=mesh['y_hi'=2,'z'=8,'core'=2,'y_lo'=4,'x'=4] {'y_hi','core'}, dimensions={0} | all-to-all | bytes 294912 | tf_op jit(solution)/shard_map/all_to_all | solution.py:175
  20.7 1.1 broadcast_in_dim.8
  21.8 0.0 copy-start
  21.8 8.6 %all-to-all-start.1 = ((bf16[8,2,48,768]{3,2,1,0:T(8,128)(2,1)}), bf16[8,2,48,768]{3,2,1,0:T(8,128)(2,1)S(1)}, u32[]{:S(2)}, u32[]{:S(2)}) async-start(bf16[8,2,48,768]{3,2,1,0:T(8,128)(2,1)} %broadcast_in_dim.8), calls=%async_computation.1 | async-start | bytes 2359296 | tf_op jit(solution)/shard_map/all_to_all | solution.py:175
  30.4 0.0 copy-done
  30.4 2.0 %collective-permute-start = (bf16[384,768]{1,0:T(8,128)(2,1)S(1)}, bf16[384,768]{1,0:T(8,128)(2,1)S(1)}, u32[]{:S(2)}, u32[]{:S(2)}) collective-permute-start(bf16[384,768]{1,0:T(8,128)(2,1)S(1)} %bitcast.4), channel_id=1, source_target_pairs={{0,256},{256,0},{1,257},{257,1},{2,258},{258,2},{3,259},{259,3},{4... | collective-permute-start | bytes 1769480 | tf_op jit(solution)/shard_map/ppermute | solution.py:171
  32.4 23.4 %collective-permute-done.theirs_ref = bf16[384,768]{1,0:T(8,128)(2,1)S(1)} collective-permute-done((bf16[384,768]{1,0:T(8,128)(2,1)S(1)}, bf16[384,768]{1,0:T(8,128)(2,1)S(1)}, u32[]{:S(2)}, u32[]{:S(2)}) %collective-permute-start) | collective-permute-done | bytes 589856 | tf_op jit(solution)/shard_map/ppermute | solution.py:171
  55.8 6.7 %all-to-all-done.1.own_ref = bf16[8,2,48,768]{3,2,1,0:T(8,128)(2,1)S(1)} async-done(((bf16[8,2,48,768]{3,2,1,0:T(8,128)(2,1)}), bf16[8,2,48,768]{3,2,1,0:T(8,128)(2,1)S(1)}, u32[]{:S(2)}, u32[]{:S(2)}) %all-to-all-start.1) | async-done | bytes 1179680 | tf_op jit(solution)/shard_map/all_to_all | solution.py:175
  62.5 2.5 %collective-permute-start.1 = (bf16[8,2,48,768]{3,2,1,0:T(8,128)(2,1)S(1)}, bf16[8,2,48,768]{3,2,1,0:T(8,128)(2,1)S(1)}, u32[]{:S(2)}, u32[]{:S(2)}) collective-permute-start(bf16[8,2,48,768]{3,2,1,0:T(8,128)(2,1)S(1)} %all-to-all-done.1.own_ref), channel_id=1, source_target_pairs={{0,16},{16,0},{1,17},{17,1},{2,18},{18,2},{3,19},{19,3},{4,20},{20... | collective-permute-start | bytes 3538952 | tf_op jit(solution)/shard_map/ppermute | solution.py:171
  65.0 2.5 %collective-permute-done.1.sib_ref = bf16[8,2,48,768]{3,2,1,0:T(8,128)(2,1)S(1)} collective-permute-done((bf16[8,2,48,768]{3,2,1,0:T(8,128)(2,1)S(1)}, bf16[8,2,48,768]{3,2,1,0:T(8,128)(2,1)S(1)}, u32[]{:S(2)}, u32[]{:S(2)}) %collective-permute-start.1) | collective-permute-done | bytes 1179680 | tf_op jit(solution)/shard_map/ppermute | solution.py:171
  67.5 7.5 %work.1 = bf16[4,2,592,128]{3,2,1,0:T(8,128)(2,1)S(1)} custom-call(bf16[384,768]{1,0:T(8,128)(2,1)S(1)} %bitcast.5, bf16[384,768]{1,0:T(8,128)(2,1)S(1)} %collective-permute-done.theirs_ref, bf16[8,2,48,768]{3,2,1,0:T(8,128)(2,1)S(1)} %all-to-all-done.1.own_ref, bf16[8,2,48,768]{3,2,1,0:T(8,128)(2,1)S(1)} %collective-permute-done.1.sib_ref), custom_call_target="tpu_custom_call" | custom-call | tf_op jit(solution)/shard_map/work/pallas_call | solution.py:113
  75.0 20.2 %all_to_all.21.got_ref = bf16[4,2,592,128]{3,2,1,0:T(8,128)(2,1)} all-to-all(bf16[4,2,592,128]{3,2,1,0:T(8,128)(2,1)S(1)} %work.1), channel_id=1, replica_groups=mesh['y_hi'=2,'z'=8,'core'=2,'y_lo'=4,'x'=4] {'x'}, dimensions={0} | all-to-all | bytes 2424832 | tf_op jit(solution)/shard_map/all_to_all | solution.py:175
  95.2 2.3 %middle.1 = bf16[8,160,128]{2,1,0:T(8,128)(2,1)} custom-call(bf16[4,2,592,128]{3,2,1,0:T(8,128)(2,1)} %all_to_all.21.got_ref), custom_call_target="tpu_custom_call" | custom-call | tf_op jit(solution)/shard_map/middle/pallas_call | solution.py:136
  97.5 15.1 %all_to_all.22.got_ref = bf16[8,160,128]{2,1,0:T(8,128)(2,1)} all-to-all(bf16[8,160,128]{2,1,0:T(8,128)(2,1)} %middle.1), channel_id=1, replica_groups=mesh['y_hi'=2,'z'=8,'core'=2,'y_lo'=4,'x'=4] {'y_hi','y_lo'}, dimensions={0} | all-to-all | bytes 655360 | tf_op jit(solution)/shard_map/all_to_all | solution.py:175
  112.6 1.7 %close.1 = (f32[2]{0:T(128)}, f32[2,48,192]{2,1,0:T(8,128)}) custom-call(bf16[8,160,128]{2,1,0:T(8,128)(2,1)} %all_to_all.22.got_ref), custom_call_target="tpu_custom_call" | custom-call | tf_op jit(solution)/shard_map/close/pallas_call | solution.py:158
Async XLA Ops:
  21.8 8.6 %copy-start = (bf16[2,768,192]{1,2,0:T(8,128)(2,1)S(1)}, bf16[2,768,192]{1,2,0:T(8,128)(2,1)}, u32[]{:S(2)}) copy-start(bf16[2,768,192]{1,2,0:T(8,128)(2,1)} %param.3) | copy-start | bytes 1769476
  21.8 40.6 %all-to-all-start.1 = ((bf16[8,2,48,768]{3,2,1,0:T(8,128)(2,1)}), bf16[8,2,48,768]{3,2,1,0:T(8,128)(2,1)S(1)}, u32[]{:S(2)}, u32[]{:S(2)}) async-start(bf16[8,2,48,768]{3,2,1,0:T(8,128)(2,1)} %broadcast_in_dim.8), calls=%async_computation.1 | async-start | bytes 2359296 | tf_op jit(solution)/shard_map/all_to_all | solution.py:175
  30.4 25.4 %collective-permute-start = (bf16[384,768]{1,0:T(8,128)(2,1)S(1)}, bf16[384,768]{1,0:T(8,128)(2,1)S(1)}, u32[]{:S(2)}, u32[]{:S(2)}) collective-permute-start(bf16[384,768]{1,0:T(8,128)(2,1)S(1)} %bitcast.4), channel_id=1, source_target_pairs={{0,256},{256,0},{1,257},{257,1},{2,258},{258,2},{3,259},{259,3},{4... | collective-permute-start | bytes 1769480 | tf_op jit(solution)/shard_map/ppermute | solution.py:171
  62.5 5.0 %collective-permute-start.1 = (bf16[8,2,48,768]{3,2,1,0:T(8,128)(2,1)S(1)}, bf16[8,2,48,768]{3,2,1,0:T(8,128)(2,1)S(1)}, u32[]{:S(2)}, u32[]{:S(2)}) collective-permute-start(bf16[8,2,48,768]{3,2,1,0:T(8,128)(2,1)S(1)} %all-to-all-done.1.own_ref), channel_id=1, source_target_pairs={{0,16},{16,0},{1,17},{17,1},{2,18},{18,2},{3,19},{19,3},{4,20},{20... | collective-permute-start | bytes 3538952 | tf_op jit(solution)/shard_map/ppermute | solution.py:171

commit v3 on v2

v3 whole, which is shorter than its diff:
```python
import jax
import jax.numpy as jnp
from jax import lax
from jax.experimental import pallas as pl
from jax.experimental.pallas import tpu as pltpu
from jax.sharding import Mesh
from jax.sharding import PartitionSpec as P

M = 768
NOCC = 192
NCHOL = 256
WALKER = ("y_hi", "z", "core")
CHOL = ("y_lo", "x")
ROWS = 24
BLOCK = 2 * ROWS
WPER = 2
QUARTER = 4
CHUNK = QUARTER * NOCC
SHARE = WPER * NOCC // 4
NWALK = 2 * WPER
DATA = 3 * BLOCK
CARRY = 16
VMEM_LIMIT = 32 * 1024 * 1024
SMALL_LIMIT = 16 * 1024 * 1024


def whole():
    return pl.BlockSpec(memory_space=pltpu.VMEM)


def pack_kernel(chol_ref, out_ref):
    for q in range(4):
        for k in range(0, QUARTER, 2):
            first = q * QUARTER + k
            pair = jnp.concatenate([chol_ref[first], chol_ref[first + 1]], axis=1)
            out_ref[q, :, k * NOCC : (k + 2) * NOCC] = pair


def pack(chol):
    return pl.pallas_call(
        pack_kernel,
        out_shape=jax.ShapeDtypeStruct((4, ROWS, CHUNK), jnp.bfloat16),
        in_specs=[whole()],
        out_specs=whole(),
        compiler_params=pltpu.CompilerParams(vmem_limit_bytes=SMALL_LIMIT),
        name="pack",
    )(chol)


def split3(value):
    high = value.astype(jnp.bfloat16).astype(jnp.float32)
    left = value - high
    mid = left.astype(jnp.bfloat16).astype(jnp.float32)
    return high, mid, left - mid


def carry(values):
    row = lax.broadcasted_iota(jnp.int32, (CARRY, 128), 0)
    out = jnp.zeros((CARRY, 128), jnp.float32)
    for n, value in enumerate(values):
        filled = jnp.broadcast_to(value, (CARRY, 128))
        for p, part in enumerate(split3(filled)):
            out = jnp.where(row == 3 * n + p, part, out)
    return out.astype(jnp.bfloat16)


def carried(rows, n):
    return rows[3 * n : 3 * n + 1] + rows[3 * n + 1 : 3 * n + 2] + rows[3 * n + 2 : 3 * n + 3]


def contract(greens, x_ref, stack_ref, energy_ref):
    half = M // 2
    x = jnp.concatenate([x_ref[:, side].reshape(half, CHUNK) for side in range(2)], axis=0)
    diagonal = lax.broadcasted_iota(jnp.int32, (NOCC, NOCC), 0) == lax.broadcasted_iota(jnp.int32, (NOCC, NOCC), 1)
    for g, green in enumerate(greens):
        part = jnp.dot(green[...], x, preferred_element_type=jnp.float32)
        for w in range(WPER):
            n = g * WPER + w
            walker = part[w * NOCC : (w + 1) * NOCC]
            for q in range(QUARTER):
                stack_ref[n, q * NOCC : (q + 1) * NOCC, :] = walker[:, q * NOCC : (q + 1) * NOCC].astype(jnp.bfloat16)
            trace = jnp.dot(walker.astype(jnp.bfloat16), stack_ref[n], preferred_element_type=jnp.float32)
            value = jnp.sum(jnp.where(diagonal, trace, 0.0))
            energy_ref[n : n + 1, :] = jnp.full((1, 128), value, jnp.float32)


def first_kernel(mine_ref, s0_ref, s1_ref, s2_ref, s3_ref, x_ref, stack_ref, energy_ref, other_ref):
    here = lax.axis_index("x")
    for step, piece in enumerate((s0_ref, s1_ref, s2_ref, s3_ref)):
        base = lax.rem(here + step, 4) * SHARE
        other_ref[pl.ds(pl.multiple_of(base, 16), SHARE), :] = piece[...]
    contract((mine_ref, other_ref), x_ref, stack_ref, energy_ref)


def second_kernel(mine_ref, other_ref, x_ref, stack_ref, energy_ref):
    contract((mine_ref, other_ref), x_ref, stack_ref, energy_ref)


def params():
    return pltpu.CompilerParams(vmem_limit_bytes=VMEM_LIMIT)


STACKED = (
    jax.ShapeDtypeStruct((NWALK, CHUNK, NOCC), jnp.bfloat16),
    jax.ShapeDtypeStruct((NWALK, 128), jnp.float32),
)


def first(*args):
    return pl.pallas_call(
        first_kernel,
        out_shape=(*STACKED, jax.ShapeDtypeStruct((WPER * NOCC, M), jnp.bfloat16)),
        in_specs=[whole()] * len(args),
        out_specs=(whole(),) * 3,
        compiler_params=params(),
        name="first",
    )(*args)


def second(*args):
    return pl.pallas_call(
        second_kernel,
        out_shape=STACKED,
        in_specs=[whole()] * len(args),
        out_specs=(whole(),) * 2,
        compiler_params=params(),
        name="second",
    )(*args)


def spread_kernel(own_ref, sib_ref, stack0_ref, stack1_ref, e0_ref, e1_ref, pay_ref):
    side = lax.axis_index("y_hi")
    half = M // 2
    energies = e0_ref[...] + e1_ref[...]
    for g in range(2):
        y = side if g == 0 else 1 - side
        for m in range(2):
            grads = []
            for w in range(WPER):
                n = g * WPER + w
                grad = jnp.dot(own_ref[:, m].reshape(half, CHUNK), stack0_ref[n], preferred_element_type=jnp.float32)
                grads.append(
                    grad + jnp.dot(sib_ref[:, m].reshape(half, CHUNK), stack1_ref[n], preferred_element_type=jnp.float32)
                )
            rest = jnp.concatenate([grads[0][:, 128:], grads[1][:, 128:]], axis=1).astype(jnp.bfloat16)
            parts = [grad[:, :128].astype(jnp.bfloat16) for grad in grads] + [rest]
            for b in range(8):
                x, y_lo = b % 4, m * 2 + b // 4
                for p, part in enumerate(parts):
                    base = y_lo * DATA + p * BLOCK
                    pay_ref[x, y, base : base + BLOCK, :] = part[b * BLOCK : (b + 1) * BLOCK]
        rows = carry([energies[g * WPER + w : g * WPER + w + 1, :1] for w in range(WPER)])
        for x in range(4):
            pay_ref[x, y, 4 * DATA : 4 * DATA + CARRY, :] = rows


def spread(*args):
    return pl.pallas_call(
        spread_kernel,
        out_shape=jax.ShapeDtypeStruct((4, 2, 4 * DATA + CARRY, 128), jnp.bfloat16),
        in_specs=[whole()] * len(args),
        out_specs=whole(),
        compiler_params=params(),
        name="spread",
    )(*args)


def middle_kernel(got_ref, pay_ref):
    for y in range(2):
        total = got_ref[0, y].astype(jnp.float32)
        for x in range(1, 4):
            total = total + got_ref[x, y].astype(jnp.float32)
        rows = carry([carried(total[4 * DATA :], w)[:, :1] for w in range(WPER)])
        for y_lo in range(4):
            pay_ref[y * 4 + y_lo, :DATA, :] = total[y_lo * DATA : (y_lo + 1) * DATA].astype(jnp.bfloat16)
            pay_ref[y * 4 + y_lo, DATA:, :] = rows


def middle(*args):
    return pl.pallas_call(
        middle_kernel,
        out_shape=jax.ShapeDtypeStruct((8, DATA + CARRY, 128), jnp.bfloat16),
        in_specs=[whole()] * len(args),
        out_specs=whole(),
        compiler_params=pltpu.CompilerParams(vmem_limit_bytes=SMALL_LIMIT),
        name="middle",
    )(*args)


def close_kernel(got_ref, energy_ref, gradient_ref):
    escale = 1.0 / (NCHOL * NOCC)
    gscale = 1.0 / NCHOL**0.5
    total = got_ref[0].astype(jnp.float32)
    for n in range(1, 8):
        total = total + got_ref[n].astype(jnp.float32)
    for w in range(WPER):
        rest = total[2 * BLOCK : DATA, 64 * w : 64 * (w + 1)]
        gradient_ref[w] = jnp.concatenate([total[BLOCK * w : BLOCK * (w + 1)], rest], axis=1) * gscale
        energy_ref[w] = carried(total[DATA:], w)[0, 0] * escale


def close(got):
    return pl.pallas_call(
        close_kernel,
        out_shape=(
            jax.ShapeDtypeStruct((WPER,), jnp.float32),
            jax.ShapeDtypeStruct((WPER, BLOCK, NOCC), jnp.float32),
        ),
        in_specs=[whole()],
        out_specs=(pl.BlockSpec(memory_space=pltpu.SMEM), whole()),
        compiler_params=pltpu.CompilerParams(vmem_limit_bytes=SMALL_LIMIT),
        name="close",
    )(got)


def swap(value, axis):
    return lax.ppermute(value, axis, [(0, 1), (1, 0)])


def exchange(value, axes):
    return lax.all_to_all(value, axes, split_axis=0, concat_axis=0, tiled=True)


def per_device(chol_vectors, green):
    turned = jnp.swapaxes(green, 1, 2).reshape(WPER * NOCC, M)
    share = lax.dynamic_index_in_dim(turned.reshape(4, SHARE, M), lax.axis_index("x"), 0, keepdims=False)
    packed = exchange(pack(chol_vectors), ("y_hi", "core"))
    packed, share = lax.optimization_barrier((packed, share))
    share = swap(share, "y_hi")
    shares = [share] + [lax.ppermute(share, "x", [((x + step) % 4, x) for x in range(4)]) for step in (1, 2, 3)]
    block = packed.reshape(2, BLOCK, CHUNK)
    own = exchange(jnp.broadcast_to(block[None], (8, *block.shape)), "z")
    own, shares = lax.optimization_barrier((own, shares))
    sib = swap(own, "core")
    own, sib = (value.reshape(8, 2, BLOCK, CHUNK) for value in (own, sib))
    stack0, e0, other = first(turned, *shares, own)
    stack1, e1 = second(turned, other, sib)
    got = exchange(middle(exchange(spread(own, sib, stack0, stack1, e0, e1), "x")), ("y_hi", "y_lo"))
    return close(got)


def solution(mesh):
    torus = Mesh(
        mesh.devices.reshape(2, 8, 2, 4, 4),
        ("y_hi", "z", "core", "y_lo", "x"),
    )
    return jax.shard_map(
        per_device,
        mesh=torus,
        in_specs=(P(CHOL, WALKER, None), P(WALKER, None, None)),
        out_specs=(P(WALKER), P(WALKER, CHOL, None)),
        check_vma=False,
    )
```

time: 116 us -> 108 us (0.931)
  starting transfers between devices: 13.1 us -> 34.2 us
  blocking collectives: 53.7 us -> 34.3 us
  waiting for transfers between devices: 32.5 us -> 26 us
  Pallas kernels: 13.2 us -> 8.63 us
  local copies, waits for them, and re-layouts: 1.1 us -> 2.95 us
    all_to_all x3 -> x2, blocking collectives: 53.7 us -> 34.3 us  [exchange(): return lax.all_to_all(value, axes, split_axis=0, concat_axis=0, tiled=True)]
    ppermute x2, waiting for transfers between devices: 25.8 us -> 8.4 us  [swap(): return lax.ppermute(value, axis, [(0, 1), (1, 0)])]
    ppermute x0 -> x3, starting transfers between devices: none -> 10.5 us  [per_device(): lax.ppermute(share, 'x', [((x + step) % 4, x) for x in range(4)])]
    all_to_all x1 -> x2, starting transfers between devices: 8.59 us -> 18.8 us  [exchange(): return lax.all_to_all(value, axes, split_axis=0, concat_axis=0, tiled=True)]
    all_to_all x1 -> x2, waiting for transfers between devices: 6.66 us -> 13.2 us  [exchange(): return lax.all_to_all(value, axes, split_axis=0, concat_axis=0, tiled=True)]
    ppermute x0 -> x3, waiting for transfers between devices: none -> 4.39 us  [per_device(): lax.ppermute(share, 'x', [((x + step) % 4, x) for x in range(4)])]
    pallas_call x1, Pallas kernels: 2.28 us -> 0.25 us  [middle(): pl.pallas_call(middle_kernel, out_shape=jax.ShapeDtypeStruct((8, DATA + C...]
    pallas_call x1 -> x3, Pallas kernels: 7.55 us -> 6.88 us  [the longest x1 2.69 us: spread(): pl.pallas_call(spread_kernel, out_shape=jax.ShapeDtypeStruct((4, 2, 4 * D...]
  transfers between devices with their start and end apart: 3 -> 7, of which waited for: 3 -> 6; matrix products, arithmetic and copies ran while one was open for 0% -> 1% of each run, Pallas kernels for 0% -> 2%
where the time goes in v3:
time: 108 us; the launch traced here: 107 us
  blocking collectives  34.3 us (32%)
  starting transfers between devices  34.2 us (32%)
  waiting for transfers between devices  26 us (24%)
  Pallas kernels  8.63 us (8%)
  local copies, waits for them, and re-layouts  2.95 us (3%)
    all_to_all x2, blocking collectives, exchange(): return lax.all_to_all(value, axes, split_axis=0, concat_axis=0, tiled=True)  34.3 us
    all_to_all x2, starting transfers between devices, exchange(): return lax.all_to_all(value, axes, split_axis=0, concat_axis=0, tiled=True)  18.8 us
    all_to_all x2, waiting for transfers between devices, exchange(): return lax.all_to_all(value, axes, split_axis=0, concat_axis=0, tiled=True)  13.2 us
    ppermute x3, starting transfers between devices, per_device(): lax.ppermute(share, 'x', [((x + step) % 4, x) for x in range(4)])  10.5 us
    ppermute x2, waiting for transfers between devices, swap(): return lax.ppermute(value, axis, [(0, 1), (1, 0)])  8.4 us
    ppermute x2, starting transfers between devices, swap(): return lax.ppermute(value, axis, [(0, 1), (1, 0)])  4.86 us
    ppermute x3, waiting for transfers between devices, per_device(): lax.ppermute(share, 'x', [((x + step) % 4, x) for x in range(4)])  4.39 us
    pallas_call x1, Pallas kernels, spread(): pl.pallas_call(spread_kernel, out_shape=jax.ShapeDtypeStruct((4, 2, 4 * D...  2.69 us
  transfers between devices with their start and end apart: 7, of which 6 were waited for; matrix products, arithmetic and copies ran while one was open for 1% of the time, Pallas kernels for 2%

profile of v3, /device:TPU:1, one launch (start us, length us, event | category | flops | bytes accessed | tf_op | source)
XLA Modules:
  0.0 106.7 jit_solution(13434291738071651153)
XLA Ops:
  0.6 0.0 copy-start.1
  0.6 0.9 copy-done.1
  1.6 0.8 pack.1
  2.3 10.2 %all-to-all-start = ((bf16[4,24,768]{2,1,0:T(8,128)(2,1)}), bf16[4,24,768]{2,1,0:T(8,128)(2,1)S(1)}, u32[]{:S(2)}, u32[]{:S(2)}) async-start(bf16[4,24,768]{2,1,0:T(8,128)(2,1)} %pack.1), calls=%async_computation | async-start | bytes 294912 | tf_op jit(solution)/shard_map/all_to_all | solution.py:221
  12.5 0.9 dynamic-slice_bitcast_fusion
  13.4 6.7 %all-to-all-done = bf16[4,24,768]{2,1,0:T(8,128)(2,1)S(1)} async-done(((bf16[4,24,768]{2,1,0:T(8,128)(2,1)}), bf16[4,24,768]{2,1,0:T(8,128)(2,1)S(1)}, u32[]{:S(2)}, u32[]{:S(2)}) %all-to-all-start) | async-done | bytes 147488 | tf_op jit(solution)/shard_map/all_to_all | solution.py:221
  20.1 1.1 %broadcast_in_dim.8 = bf16[8,2,48,768]{3,2,1,0:T(8,128)(2,1)} broadcast(bf16[2,48,768]{2,1,0:T(8,128)(2,1)S(1)} %bitcast.11), dimensions={1,2,3} | broadcast | bytes 1327104 | tf_op jit(solution)/shard_map/broadcast_in_dim | solution.py:232
  21.2 0.0 copy-start
  21.2 8.6 %all-to-all-start.1 = ((bf16[8,2,48,768]{3,2,1,0:T(8,128)(2,1)}), bf16[8,2,48,768]{3,2,1,0:T(8,128)(2,1)S(1)}, u32[]{:S(2)}, u32[]{:S(2)}) async-start(bf16[8,2,48,768]{3,2,1,0:T(8,128)(2,1)} %broadcast_in_dim.8), calls=%async_computation.1 | async-start | bytes 2359296 | tf_op jit(solution)/shard_map/all_to_all | solution.py:221
  29.8 2.5 %collective-permute-start = (bf16[96,768]{1,0:T(8,128)(2,1)S(1)}, bf16[96,768]{1,0:T(8,128)(2,1)S(1)}, u32[]{:S(2)}, u32[]{:S(2)}) collective-permute-start(bf16[96,768]{1,0:T(8,128)(2,1)S(1)} %dynamic-slice_bitcast_fusion), channel_id=1, source_target_pairs={{0,256},{256,0},{1,257},{257,1},{2,258},{258,2},{3,259},{259,3},{4... | collective-permute-start | bytes 442376 | tf_op jit(solution)/shard_map/ppermute | solution.py:217
  32.3 8.1 %collective-permute-done.s0_ref = bf16[96,768]{1,0:T(8,128)(2,1)S(1)} collective-permute-done((bf16[96,768]{1,0:T(8,128)(2,1)S(1)}, bf16[96,768]{1,0:T(8,128)(2,1)S(1)}, u32[]{:S(2)}, u32[]{:S(2)}) %collective-permute-start) | collective-permute-done | bytes 147488 | tf_op jit(solution)/shard_map/ppermute | solution.py:217
  40.4 3.1 %collective-permute-start.3 = (bf16[96,768]{1,0:T(8,128)(2,1)S(1)}, bf16[96,768]{1,0:T(8,128)(2,1)S(1)}, u32[]{:S(2)}, u32[]{:S(2)}) collective-permute-start(bf16[96,768]{1,0:T(8,128)(2,1)S(1)} %collective-permute-done.s0_ref), channel_id=1, source_target_pairs={{3,0},{0,1},{1,2},{2,3},{7,4},{4,5},{5,6},{6,7},{11,8},{8,9},{9,10... | collective-permute-start | bytes 442376 | tf_op jit(solution)/shard_map/ppermute | solution.py:230
  43.5 4.4 %collective-permute-start.2 = (bf16[96,768]{1,0:T(8,128)(2,1)S(1)}, bf16[96,768]{1,0:T(8,128)(2,1)S(1)}, u32[]{:S(2)}, u32[]{:S(2)}) collective-permute-start(bf16[96,768]{1,0:T(8,128)(2,1)S(1)} %collective-permute-done.s0_ref), channel_id=1, source_target_pairs={{2,0},{3,1},{0,2},{1,3},{6,4},{7,5},{4,6},{5,7},{10,8},{11,9},{8,1... | collective-permute-start | bytes 442376 | tf_op jit(solution)/shard_map/ppermute | solution.py:230
  47.9 3.1 %collective-permute-start.1 = (bf16[96,768]{1,0:T(8,128)(2,1)S(1)}, bf16[96,768]{1,0:T(8,128)(2,1)S(1)}, u32[]{:S(2)}, u32[]{:S(2)}) collective-permute-start(bf16[96,768]{1,0:T(8,128)(2,1)S(1)} %collective-permute-done.s0_ref), channel_id=1, source_target_pairs={{1,0},{2,1},{3,2},{0,3},{5,4},{6,5},{7,6},{4,7},{9,8},{10,9},{11,1... | collective-permute-start | bytes 442376 | tf_op jit(solution)/shard_map/ppermute | solution.py:230
  50.9 0.0 collective-permute-done.3.s3_ref
  51.0 0.2 collective-permute-done.2.s2_ref
  51.2 4.2 %collective-permute-done.1.s1_ref = bf16[96,768]{1,0:T(8,128)(2,1)S(1)} collective-permute-done((bf16[96,768]{1,0:T(8,128)(2,1)S(1)}, bf16[96,768]{1,0:T(8,128)(2,1)S(1)}, u32[]{:S(2)}, u32[]{:S(2)}) %collective-permute-start.1) | collective-permute-done | bytes 147488 | tf_op jit(solution)/shard_map/ppermute | solution.py:230
  55.4 6.5 %all-to-all-done.1.x_ref.own_ref = bf16[8,2,48,768]{3,2,1,0:T(8,128)(2,1)S(1)} async-done(((bf16[8,2,48,768]{3,2,1,0:T(8,128)(2,1)}), bf16[8,2,48,768]{3,2,1,0:T(8,128)(2,1)S(1)}, u32[]{:S(2)}, u32[]{:S(2)}) %all-to-all-start.1) | async-done | bytes 1179680 | tf_op jit(solution)/shard_map/all_to_all | solution.py:221
  61.8 2.4 %collective-permute-start.4 = (bf16[8,2,48,768]{3,2,1,0:T(8,128)(2,1)S(1)}, bf16[8,2,48,768]{3,2,1,0:T(8,128)(2,1)S(1)}, u32[]{:S(2)}, u32[]{:S(2)}) collective-permute-start(bf16[8,2,48,768]{3,2,1,0:T(8,128)(2,1)S(1)} %all-to-all-done.1.x_ref.own_ref), channel_id=1, source_target_pairs={{0,16},{16,0},{1,17},{17,1},{2,18},{18,2},{3,19},{19,3},{4,20},{20... | collective-permute-start | bytes 3538952 | tf_op jit(solution)/shard_map/ppermute | solution.py:217
  64.2 0.0 copy-done
  64.3 2.1 %first.1 = (bf16[4,768,192]{2,1,0:T(8,128)(2,1)S(1)}, f32[4,128]{1,0:T(4,128)S(1)}, bf16[384,768]{1,0:T(8,128)(2,1)S(1)}) custom-call(bf16[384,768]{1,0:T(8,128)(2,1)S(1)} %bitcast.9, bf16[96,768]{1,0:T(8,128)(2,1)S(1)} %collective-permute-done.s0_ref, bf16[96,768]{1,0:T(8,128)(2,1)S(1)} %collective-permute-done.1.s1_ref, ...), custom_call_target="tpu_custom_call" | custom-call | tf_op jit(solution)/shard_map/first/pallas_call | solution.py:110
  66.4 0.3 collective-permute-done.4.x_ref.sib_ref
  66.7 2.1 %second.1 = (bf16[4,768,192]{2,1,0:T(8,128)(2,1)S(1)}, f32[4,128]{1,0:T(4,128)S(1)}) custom-call(bf16[384,768]{1,0:T(8,128)(2,1)S(1)} %bitcast.10, bf16[384,768]{1,0:T(8,128)(2,1)S(1)} %get-tuple-element.22.other_ref, bf16[8,2,48,768]{3,2,1,0:T(8,128)(2,1)S(1)} %collective-permute-done.4.x_ref.sib_ref), custom_call_target="tpu_custom_call" | custom-call | tf_op jit(solution)/shard_map/second/pallas_call | solution.py:121
  68.8 2.7 %spread.1 = bf16[4,2,592,128]{3,2,1,0:T(8,128)(2,1)S(1)} custom-call(bf16[8,2,48,768]{3,2,1,0:T(8,128)(2,1)S(1)} %all-to-all-done.1.x_ref.own_ref, bf16[8,2,48,768]{3,2,1,0:T(8,128)(2,1)S(1)} %collective-permute-done.4.x_ref.sib_ref, bf16[4,768,192]{2,1,0:T(8,128)(2,1)S(1)} %get-tuple-element.21.stack0_ref, ...), custom_call_target="tpu_custom_call" | custom-call | tf_op jit(solution)/shard_map/spread/pallas_call | solution.py:158
  71.5 20.1 %all_to_all.20.got_ref = bf16[4,2,592,128]{3,2,1,0:T(8,128)(2,1)S(1)} all-to-all(bf16[4,2,592,128]{3,2,1,0:T(8,128)(2,1)S(1)} %spread.1), channel_id=1, replica_groups=mesh['y_hi'=2,'z'=8,'core'=2,'y_lo'=4,'x'=4] {'x'}, dimensions={0} | all-to-all | bytes 2424832 | tf_op jit(solution)/shard_map/all_to_all | solution.py:221
  91.6 0.3 middle.1
  91.8 14.2 %all_to_all.21.got_ref = bf16[8,160,128]{2,1,0:T(8,128)(2,1)S(1)} all-to-all(bf16[8,160,128]{2,1,0:T(8,128)(2,1)S(1)} %middle.1), channel_id=1, replica_groups=mesh['y_hi'=2,'z'=8,'core'=2,'y_lo'=4,'x'=4] {'y_hi','y_lo'}, dimensions={0} | all-to-all | bytes 655360 | tf_op jit(solution)/shard_map/all_to_all | solution.py:221
  106.0 0.7 close.1
Async XLA Ops:
  0.6 0.9 copy-start.1
  2.3 17.8 %all-to-all-start = ((bf16[4,24,768]{2,1,0:T(8,128)(2,1)}), bf16[4,24,768]{2,1,0:T(8,128)(2,1)S(1)}, u32[]{:S(2)}, u32[]{:S(2)}) async-start(bf16[4,24,768]{2,1,0:T(8,128)(2,1)} %pack.1), calls=%async_computation | async-start | bytes 294912 | tf_op jit(solution)/shard_map/all_to_all | solution.py:221
  21.2 43.0 %copy-start = (bf16[2,768,192]{1,2,0:T(8,128)(2,1)S(1)}, bf16[2,768,192]{1,2,0:T(8,128)(2,1)}, u32[]{:S(2)}) copy-start(bf16[2,768,192]{1,2,0:T(8,128)(2,1)} %param.3) | copy-start | bytes 1769476
  21.2 40.6 %all-to-all-start.1 = ((bf16[8,2,48,768]{3,2,1,0:T(8,128)(2,1)}), bf16[8,2,48,768]{3,2,1,0:T(8,128)(2,1)S(1)}, u32[]{:S(2)}, u32[]{:S(2)}) async-start(bf16[8,2,48,768]{3,2,1,0:T(8,128)(2,1)} %broadcast_in_dim.8), calls=%async_computation.1 | async-start | bytes 2359296 | tf_op jit(solution)/shard_map/all_to_all | solution.py:221
  29.8 10.6 %collective-permute-start = (bf16[96,768]{1,0:T(8,128)(2,1)S(1)}, bf16[96,768]{1,0:T(8,128)(2,1)S(1)}, u32[]{:S(2)}, u32[]{:S(2)}) collective-permute-start(bf16[96,768]{1,0:T(8,128)(2,1)S(1)} %dynamic-slice_bitcast_fusion), channel_id=1, source_target_pairs={{0,256},{256,0},{1,257},{257,1},{2,258},{258,2},{3,259},{259,3},{4... | collective-permute-start | bytes 442376 | tf_op jit(solution)/shard_map/ppermute | solution.py:217
  40.4 10.6 %collective-permute-start.3 = (bf16[96,768]{1,0:T(8,128)(2,1)S(1)}, bf16[96,768]{1,0:T(8,128)(2,1)S(1)}, u32[]{:S(2)}, u32[]{:S(2)}) collective-permute-start(bf16[96,768]{1,0:T(8,128)(2,1)S(1)} %collective-permute-done.s0_ref), channel_id=1, source_target_pairs={{3,0},{0,1},{1,2},{2,3},{7,4},{4,5},{5,6},{6,7},{11,8},{8,9},{9,10... | collective-permute-start | bytes 442376 | tf_op jit(solution)/shard_map/ppermute | solution.py:230
  43.5 7.7 %collective-permute-start.2 = (bf16[96,768]{1,0:T(8,128)(2,1)S(1)}, bf16[96,768]{1,0:T(8,128)(2,1)S(1)}, u32[]{:S(2)}, u32[]{:S(2)}) collective-permute-start(bf16[96,768]{1,0:T(8,128)(2,1)S(1)} %collective-permute-done.s0_ref), channel_id=1, source_target_pairs={{2,0},{3,1},{0,2},{1,3},{6,4},{7,5},{4,6},{5,7},{10,8},{11,9},{8,1... | collective-permute-start | bytes 442376 | tf_op jit(solution)/shard_map/ppermute | solution.py:230
  47.9 7.5 %collective-permute-start.1 = (bf16[96,768]{1,0:T(8,128)(2,1)S(1)}, bf16[96,768]{1,0:T(8,128)(2,1)S(1)}, u32[]{:S(2)}, u32[]{:S(2)}) collective-permute-start(bf16[96,768]{1,0:T(8,128)(2,1)S(1)} %collective-permute-done.s0_ref), channel_id=1, source_target_pairs={{1,0},{2,1},{3,2},{0,3},{5,4},{6,5},{7,6},{4,7},{9,8},{10,9},{11,1... | collective-permute-start | bytes 442376 | tf_op jit(solution)/shard_map/ppermute | solution.py:230
  61.8 4.9 %collective-permute-start.4 = (bf16[8,2,48,768]{3,2,1,0:T(8,128)(2,1)S(1)}, bf16[8,2,48,768]{3,2,1,0:T(8,128)(2,1)S(1)}, u32[]{:S(2)}, u32[]{:S(2)}) collective-permute-start(bf16[8,2,48,768]{3,2,1,0:T(8,128)(2,1)S(1)} %all-to-all-done.1.x_ref.own_ref), channel_id=1, source_target_pairs={{0,16},{16,0},{1,17},{17,1},{2,18},{18,2},{3,19},{19,3},{4,20},{20... | collective-permute-start | bytes 3538952 | tf_op jit(solution)/shard_map/ppermute | solution.py:217

commit v4 on v3

--- a/solution.py
+++ b/solution.py
@@ -28,23 +28,23 @@
     return pl.BlockSpec(memory_space=pltpu.VMEM)
 
 
-def pack_kernel(chol_ref, out_ref):
-    for q in range(4):
+def fan_kernel(in_ref, out_ref):
+    for n in range(4):
         for k in range(0, QUARTER, 2):
-            first = q * QUARTER + k
-            pair = jnp.concatenate([chol_ref[first], chol_ref[first + 1]], axis=1)
-            out_ref[q, :, k * NOCC : (k + 2) * NOCC] = pair
-
-
-def pack(chol):
-    return pl.pallas_call(
-        pack_kernel,
-        out_shape=jax.ShapeDtypeStruct((4, ROWS, CHUNK), jnp.bfloat16),
+            pair = jnp.concatenate([in_ref[n, k], in_ref[n, k + 1]], axis=1)
+            for z in range(8):
+                out_ref[z, n, :, k * NOCC : (k + 2) * NOCC] = pair
+
+
+def fan(quarters):
+    return pl.pallas_call(
+        fan_kernel,
+        out_shape=jax.ShapeDtypeStruct((8, 4, ROWS, CHUNK), jnp.bfloat16),
         in_specs=[whole()],
         out_specs=whole(),
         compiler_params=pltpu.CompilerParams(vmem_limit_bytes=SMALL_LIMIT),
-        name="pack",
-    )(chol)
+        name="fan",
+    )(quarters)
 
 
 def split3(value):
@@ -84,15 +84,7 @@
             energy_ref[n : n + 1, :] = jnp.full((1, 128), value, jnp.float32)
 
 
-def first_kernel(mine_ref, s0_ref, s1_ref, s2_ref, s3_ref, x_ref, stack_ref, energy_ref, other_ref):
-    here = lax.axis_index("x")
-    for step, piece in enumerate((s0_ref, s1_ref, s2_ref, s3_ref)):
-        base = lax.rem(here + step, 4) * SHARE
-        other_ref[pl.ds(pl.multiple_of(base, 16), SHARE), :] = piece[...]
-    contract((mine_ref, other_ref), x_ref, stack_ref, energy_ref)
-
-
-def second_kernel(mine_ref, other_ref, x_ref, stack_ref, energy_ref):
+def products_kernel(mine_ref, other_ref, x_ref, stack_ref, energy_ref):
     contract((mine_ref, other_ref), x_ref, stack_ref, energy_ref)
 
 
@@ -106,25 +98,14 @@
 )
 
 
-def first(*args):
-    return pl.pallas_call(
-        first_kernel,
-        out_shape=(*STACKED, jax.ShapeDtypeStruct((WPER * NOCC, M), jnp.bfloat16)),
-        in_specs=[whole()] * len(args),
-        out_specs=(whole(),) * 3,
-        compiler_params=params(),
-        name="first",
-    )(*args)
-
-
-def second(*args):
-    return pl.pallas_call(
-        second_kernel,
+def products(*args):
+    return pl.pallas_call(
+        products_kernel,
         out_shape=STACKED,
         in_specs=[whole()] * len(args),
         out_specs=(whole(),) * 2,
         compiler_params=params(),
-        name="second",
+        name="products",
     )(*args)
 
 
@@ -224,17 +205,16 @@
 def per_device(chol_vectors, green):
     turned = jnp.swapaxes(green, 1, 2).reshape(WPER * NOCC, M)
     share = lax.dynamic_index_in_dim(turned.reshape(4, SHARE, M), lax.axis_index("x"), 0, keepdims=False)
-    packed = exchange(pack(chol_vectors), ("y_hi", "core"))
+    packed = exchange(chol_vectors.reshape(4, QUARTER, ROWS, NOCC), ("y_hi", "core"))
     packed, share = lax.optimization_barrier((packed, share))
     share = swap(share, "y_hi")
-    shares = [share] + [lax.ppermute(share, "x", [((x + step) % 4, x) for x in range(4)]) for step in (1, 2, 3)]
-    block = packed.reshape(2, BLOCK, CHUNK)
-    own = exchange(jnp.broadcast_to(block[None], (8, *block.shape)), "z")
-    own, shares = lax.optimization_barrier((own, shares))
+    other = lax.all_gather(share, "x", axis=0, tiled=True)
+    own = exchange(fan(packed), "z")
+    own, other = lax.optimization_barrier((own, other))
     sib = swap(own, "core")
     own, sib = (value.reshape(8, 2, BLOCK, CHUNK) for value in (own, sib))
-    stack0, e0, other = first(turned, *shares, own)
-    stack1, e1 = second(turned, other, sib)
+    stack0, e0 = products(turned, other, own)
+    stack1, e1 = products(turned, other, sib)
     got = exchange(middle(exchange(spread(own, sib, stack0, stack1, e0, e1), "x")), ("y_hi", "y_lo"))
     return close(got)
 

time: 108 us -> 108 us (level)
  blocking collectives: 34.3 us -> 45.7 us
  starting transfers between devices: 34.2 us -> 23.4 us
  local copies, waits for them, and re-layouts: 2.95 us -> 0.92 us
    all_gather x0 -> x1, blocking collectives: none -> 11.1 us  [per_device(): other = lax.all_gather(share, 'x', axis=0, tiled=True)]
    ppermute x3 -> x0, starting transfers between devices: 10.5 us -> none  [per_device(): lax.ppermute(share, 'x', [((x + step) % 4, x) for x in range(4)])]
    all_to_all x2, waiting for transfers between devices: 13.2 us -> 18.5 us  [exchange(): return lax.all_to_all(value, axes, split_axis=0, concat_axis=0, tiled=True)]
    ppermute x3 -> x0, waiting for transfers between devices: 4.39 us -> none  [per_device(): lax.ppermute(share, 'x', [((x + step) % 4, x) for x in range(4)])]
    broadcast_in_dim x1 -> x0, local copies, waits for them, and re-layouts: 1.11 us -> none  [per_device(): own = exchange(jnp.broadcast_to(block[None], (8, *block.shape)), 'z')]
  transfers between devices with their start and end apart: 7 -> 4, of which waited for: 6 -> 4; matrix products, arithmetic and copies ran while one was open for 1% -> 1% of each run, Pallas kernels for 2% -> 2%
where the time goes in v4:
time: 108 us; the launch traced here: 106 us
  blocking collectives  45.7 us (42%)
  waiting for transfers between devices  26.4 us (24%)
  starting transfers between devices  23.4 us (22%)
  Pallas kernels  9.03 us (8%)
    all_to_all x2, blocking collectives, exchange(): return lax.all_to_all(value, axes, split_axis=0, concat_axis=0, tiled=True)  34.6 us
    all_to_all x2, starting transfers between devices, exchange(): return lax.all_to_all(value, axes, split_axis=0, concat_axis=0, tiled=True)  18.8 us
    all_to_all x2, waiting for transfers between devices, exchange(): return lax.all_to_all(value, axes, split_axis=0, concat_axis=0, tiled=True)  18.5 us
    all_gather x1, blocking collectives, per_device(): other = lax.all_gather(share, 'x', axis=0, tiled=True)  11.1 us
    ppermute x2, waiting for transfers between devices, swap(): return lax.ppermute(value, axis, [(0, 1), (1, 0)])  7.97 us
    ppermute x2, starting transfers between devices, swap(): return lax.ppermute(value, axis, [(0, 1), (1, 0)])  4.67 us
    pallas_call x2, Pallas kernels, products(): pl.pallas_call(products_kernel, out_shape=STACKED, in_specs=[whole()] * l...  4.15 us
    pallas_call x1, Pallas kernels, spread(): pl.pallas_call(spread_kernel, out_shape=jax.ShapeDtypeStruct((4, 2, 4 * D...  2.69 us
  transfers between devices with their start and end apart: 4, of which 4 were waited for; matrix products, arithmetic and copies ran while one was open for 1% of the time, Pallas kernels for 2%

profile of v4, /device:TPU:1, one launch (start us, length us, event | category | flops | bytes accessed | tf_op | source)
XLA Modules:
  0.0 106.2 jit_solution(11537054727756581274)
XLA Ops:
  0.6 10.2 %all-to-all-start = ((bf16[4,4,24,192]{3,2,1,0:T(8,128)(2,1)}), bf16[4,4,24,192]{3,2,1,0:T(8,128)(2,1)S(1)}, u32[]{:S(2)}, u32[]{:S(2)}) async-start(bf16[4,4,24,192]{3,2,1,0:T(8,128)(2,1)} %bitcast.17), calls=%async_computation | async-start | bytes 393216 | tf_op jit(solution)/shard_map/all_to_all | solution.py:202
  10.9 0.9 dynamic-slice_bitcast_fusion
  11.8 7.5 %all-to-all-done.in_ref = bf16[4,4,24,192]{3,2,1,0:T(8,128)(2,1)S(1)} async-done(((bf16[4,4,24,192]{3,2,1,0:T(8,128)(2,1)}), bf16[4,4,24,192]{3,2,1,0:T(8,128)(2,1)S(1)}, u32[]{:S(2)}, u32[]{:S(2)}) %all-to-all-start) | async-done | bytes 147488 | tf_op jit(solution)/shard_map/all_to_all | solution.py:202
  19.2 1.2 %fan.1 = bf16[8,4,24,768]{3,2,1,0:T(8,128)(2,1)} custom-call(bf16[4,4,24,192]{3,2,1,0:T(8,128)(2,1)S(1)} %all-to-all-done.in_ref), custom_call_target="tpu_custom_call" | custom-call | tf_op jit(solution)/shard_map/fan/pallas_call | solution.py:40
  20.4 0.0 copy-start
  20.4 8.6 %all-to-all-start.1 = ((bf16[8,4,24,768]{3,2,1,0:T(8,128)(2,1)}), bf16[8,4,24,768]{3,2,1,0:T(8,128)(2,1)S(1)}, u32[]{:S(2)}, u32[]{:S(2)}) async-start(bf16[8,4,24,768]{3,2,1,0:T(8,128)(2,1)} %fan.1), calls=%async_computation.1 | async-start | bytes 2359296 | tf_op jit(solution)/shard_map/all_to_all | solution.py:202
  29.0 2.3 %collective-permute-start = (bf16[96,768]{1,0:T(8,128)(2,1)S(1)}, bf16[96,768]{1,0:T(8,128)(2,1)S(1)}, u32[]{:S(2)}, u32[]{:S(2)}) collective-permute-start(bf16[96,768]{1,0:T(8,128)(2,1)S(1)} %dynamic-slice_bitcast_fusion), channel_id=1, source_target_pairs={{0,256},{256,0},{1,257},{257,1},{2,258},{258,2},{3,259},{259,3},{4... | collective-permute-start | bytes 442376 | tf_op jit(solution)/shard_map/ppermute | solution.py:198
  31.3 7.6 %collective-permute-done = bf16[96,768]{1,0:T(8,128)(2,1)S(1)} collective-permute-done((bf16[96,768]{1,0:T(8,128)(2,1)S(1)}, bf16[96,768]{1,0:T(8,128)(2,1)S(1)}, u32[]{:S(2)}, u32[]{:S(2)}) %collective-permute-start) | collective-permute-done | bytes 147488 | tf_op jit(solution)/shard_map/ppermute | solution.py:198
  38.9 11.1 %all_gather.3.other_ref = bf16[384,768]{1,0:T(8,128)(2,1)S(1)} all-gather(bf16[96,768]{1,0:T(8,128)(2,1)S(1)} %collective-permute-done), channel_id=1, replica_groups=mesh['y_hi'=2,'z'=8,'core'=2,'y_lo'=4,'x'=4] {'x'}, dimensions={0}, use_global_device_ids=true | all-gather | bytes 737280 | tf_op jit(solution)/shard_map/all_gather | solution.py:211
  50.0 11.0 %all-to-all-done.1 = bf16[8,4,24,768]{3,2,1,0:T(8,128)(2,1)S(1)} async-done(((bf16[8,4,24,768]{3,2,1,0:T(8,128)(2,1)}), bf16[8,4,24,768]{3,2,1,0:T(8,128)(2,1)S(1)}, u32[]{:S(2)}, u32[]{:S(2)}) %all-to-all-start.1) | async-done | bytes 1179680 | tf_op jit(solution)/shard_map/all_to_all | solution.py:202
  61.0 2.4 %collective-permute-start.1 = (bf16[8,4,24,768]{3,2,1,0:T(8,128)(2,1)S(1)}, bf16[8,4,24,768]{3,2,1,0:T(8,128)(2,1)S(1)}, u32[]{:S(2)}, u32[]{:S(2)}) collective-permute-start(bf16[8,4,24,768]{3,2,1,0:T(8,128)(2,1)S(1)} %all-to-all-done.1), channel_id=1, source_target_pairs={{0,16},{16,0},{1,17},{17,1},{2,18},{18,2},{3,19},{19,3},{4,20},{20... | collective-permute-start | bytes 3538952 | tf_op jit(solution)/shard_map/ppermute | solution.py:198
  63.4 0.0 copy-done
  63.4 2.1 %products.2 = (bf16[4,768,192]{2,1,0:T(8,128)(2,1)S(1)}, f32[4,128]{1,0:T(4,128)S(1)}) custom-call(bf16[384,768]{1,0:T(8,128)(2,1)S(1)} %bitcast.15, bf16[384,768]{1,0:T(8,128)(2,1)S(1)} %all_gather.3.other_ref, bf16[8,2,48,768]{3,2,1,0:T(8,128)(2,1)S(1)} %bitcast.10), custom_call_target="tpu_custom_call" | custom-call | tf_op jit(solution)/shard_map/products/pallas_call | solution.py:102
  65.5 0.4 collective-permute-done.1
  65.9 2.1 %products.3 = (bf16[4,768,192]{2,1,0:T(8,128)(2,1)S(1)}, f32[4,128]{1,0:T(4,128)S(1)}) custom-call(bf16[384,768]{1,0:T(8,128)(2,1)S(1)} %bitcast.16, bf16[384,768]{1,0:T(8,128)(2,1)S(1)} %all_gather.3.other_ref, bf16[8,2,48,768]{3,2,1,0:T(8,128)(2,1)S(1)} %bitcast.12), custom_call_target="tpu_custom_call" | custom-call | tf_op jit(solution)/shard_map/products/pallas_call | solution.py:102
  67.9 2.7 %spread.1 = bf16[4,2,592,128]{3,2,1,0:T(8,128)(2,1)S(1)} custom-call(bf16[8,2,48,768]{3,2,1,0:T(8,128)(2,1)S(1)} %bitcast.11, bf16[8,2,48,768]{3,2,1,0:T(8,128)(2,1)S(1)} %bitcast.13, bf16[4,768,192]{2,1,0:T(8,128)(2,1)S(1)} %get-tuple-element.14.stack0_ref, bf16[4,768,192]{2,1,0:T(8,128)(2,1)S(1)} %get-tuple-element.15.stack1_ref, ...), custom_call_target="tpu_custom_call" | custom-call | tf_op jit(solution)/shard_map/spread/pallas_call | solution.py:139
  70.6 20.1 %all_to_all.20.got_ref = bf16[4,2,592,128]{3,2,1,0:T(8,128)(2,1)S(1)} all-to-all(bf16[4,2,592,128]{3,2,1,0:T(8,128)(2,1)S(1)} %spread.1), channel_id=1, replica_groups=mesh['y_hi'=2,'z'=8,'core'=2,'y_lo'=4,'x'=4] {'x'}, dimensions={0} | all-to-all | bytes 2424832 | tf_op jit(solution)/shard_map/all_to_all | solution.py:202
  90.7 0.3 middle.1
  91.0 14.5 %all_to_all.21.got_ref = bf16[8,160,128]{2,1,0:T(8,128)(2,1)S(1)} all-to-all(bf16[8,160,128]{2,1,0:T(8,128)(2,1)S(1)} %middle.1), channel_id=1, replica_groups=mesh['y_hi'=2,'z'=8,'core'=2,'y_lo'=4,'x'=4] {'y_hi','y_lo'}, dimensions={0} | all-to-all | bytes 655360 | tf_op jit(solution)/shard_map/all_to_all | solution.py:202
  105.5 0.7 close.1
Async XLA Ops:
  0.6 18.6 %all-to-all-start = ((bf16[4,4,24,192]{3,2,1,0:T(8,128)(2,1)}), bf16[4,4,24,192]{3,2,1,0:T(8,128)(2,1)S(1)}, u32[]{:S(2)}, u32[]{:S(2)}) async-start(bf16[4,4,24,192]{3,2,1,0:T(8,128)(2,1)} %bitcast.17), calls=%async_computation | async-start | bytes 393216 | tf_op jit(solution)/shard_map/all_to_all | solution.py:202
  20.4 43.0 %copy-start = (bf16[2,768,192]{1,2,0:T(8,128)(2,1)S(1)}, bf16[2,768,192]{1,2,0:T(8,128)(2,1)}, u32[]{:S(2)}) copy-start(bf16[2,768,192]{1,2,0:T(8,128)(2,1)} %param.3) | copy-start | bytes 1769476
  20.4 40.6 %all-to-all-start.1 = ((bf16[8,4,24,768]{3,2,1,0:T(8,128)(2,1)}), bf16[8,4,24,768]{3,2,1,0:T(8,128)(2,1)S(1)}, u32[]{:S(2)}, u32[]{:S(2)}) async-start(bf16[8,4,24,768]{3,2,1,0:T(8,128)(2,1)} %fan.1), calls=%async_computation.1 | async-start | bytes 2359296 | tf_op jit(solution)/shard_map/all_to_all | solution.py:202
  29.0 9.9 %collective-permute-start = (bf16[96,768]{1,0:T(8,128)(2,1)S(1)}, bf16[96,768]{1,0:T(8,128)(2,1)S(1)}, u32[]{:S(2)}, u32[]{:S(2)}) collective-permute-start(bf16[96,768]{1,0:T(8,128)(2,1)S(1)} %dynamic-slice_bitcast_fusion), channel_id=1, source_target_pairs={{0,256},{256,0},{1,257},{257,1},{2,258},{258,2},{3,259},{259,3},{4... | collective-permute-start | bytes 442376 | tf_op jit(solution)/shard_map/ppermute | solution.py:198
  61.0 4.9 %collective-permute-start.1 = (bf16[8,4,24,768]{3,2,1,0:T(8,128)(2,1)S(1)}, bf16[8,4,24,768]{3,2,1,0:T(8,128)(2,1)S(1)}, u32[]{:S(2)}, u32[]{:S(2)}) collective-permute-start(bf16[8,4,24,768]{3,2,1,0:T(8,128)(2,1)S(1)} %all-to-all-done.1), channel_id=1, source_target_pairs={{0,16},{16,0},{1,17},{17,1},{2,18},{18,2},{3,19},{19,3},{4,20},{20... | collective-permute-start | bytes 3538952 | tf_op jit(solution)/shard_map/ppermute | solution.py:198

commit v5 on v4

--- a/solution.py
+++ b/solution.py
@@ -72,16 +72,15 @@
     half = M // 2
     x = jnp.concatenate([x_ref[:, side].reshape(half, CHUNK) for side in range(2)], axis=0)
     diagonal = lax.broadcasted_iota(jnp.int32, (NOCC, NOCC), 0) == lax.broadcasted_iota(jnp.int32, (NOCC, NOCC), 1)
-    for g, green in enumerate(greens):
-        part = jnp.dot(green[...], x, preferred_element_type=jnp.float32)
-        for w in range(WPER):
-            n = g * WPER + w
-            walker = part[w * NOCC : (w + 1) * NOCC]
-            for q in range(QUARTER):
-                stack_ref[n, q * NOCC : (q + 1) * NOCC, :] = walker[:, q * NOCC : (q + 1) * NOCC].astype(jnp.bfloat16)
-            trace = jnp.dot(walker.astype(jnp.bfloat16), stack_ref[n], preferred_element_type=jnp.float32)
-            value = jnp.sum(jnp.where(diagonal, trace, 0.0))
-            energy_ref[n : n + 1, :] = jnp.full((1, 128), value, jnp.float32)
+    greens = jnp.concatenate([green[...] for green in greens], axis=0)
+    part = jnp.dot(greens, x, preferred_element_type=jnp.float32)
+    for n in range(NWALK):
+        walker = part[n * NOCC : (n + 1) * NOCC]
+        for q in range(QUARTER):
+            stack_ref[n, q * NOCC : (q + 1) * NOCC, :] = walker[:, q * NOCC : (q + 1) * NOCC].astype(jnp.bfloat16)
+        trace = jnp.dot(walker.astype(jnp.bfloat16), stack_ref[n], preferred_element_type=jnp.float32)
+        value = jnp.sum(jnp.where(diagonal, trace, 0.0))
+        energy_ref[n : n + 1, :] = jnp.full((1, 128), value, jnp.float32)
 
 
 def products_kernel(mine_ref, other_ref, x_ref, stack_ref, energy_ref):
@@ -109,7 +108,8 @@
     )(*args)
 
 
-def spread_kernel(own_ref, sib_ref, stack0_ref, stack1_ref, e0_ref, e1_ref, pay_ref):
+def spread_kernel(mine_ref, other_ref, own_ref, sib_ref, stack0_ref, e0_ref, pay_ref, stack1_ref, e1_ref):
+    contract((mine_ref, other_ref), sib_ref, stack1_ref, e1_ref)
     side = lax.axis_index("y_hi")
     half = M // 2
     energies = e0_ref[...] + e1_ref[...]
@@ -141,6 +141,7 @@
         out_shape=jax.ShapeDtypeStruct((4, 2, 4 * DATA + CARRY, 128), jnp.bfloat16),
         in_specs=[whole()] * len(args),
         out_specs=whole(),
+        scratch_shapes=[pltpu.VMEM(shape.shape, shape.dtype) for shape in STACKED],
         compiler_params=params(),
         name="spread",
     )(*args)
@@ -214,8 +215,7 @@
     sib = swap(own, "core")
     own, sib = (value.reshape(8, 2, BLOCK, CHUNK) for value in (own, sib))
     stack0, e0 = products(turned, other, own)
-    stack1, e1 = products(turned, other, sib)
-    got = exchange(middle(exchange(spread(own, sib, stack0, stack1, e0, e1), "x")), ("y_hi", "y_lo"))
+    got = exchange(middle(exchange(spread(turned, other, own, sib, stack0, e0), "x")), ("y_hi", "y_lo"))
     return close(got)
 
 

time: 108 us -> 107 us (level)
    pallas_call x2 -> x1, Pallas kernels: 4.15 us -> 2.14 us  [products(): pl.pallas_call(products_kernel, out_shape=STACKED, in_specs=[whole()] * l...]
    pallas_call x1, Pallas kernels: 2.69 us -> 4.55 us  [spread(): pl.pallas_call(spread_kernel, out_shape=jax.ShapeDtypeStruct((4, 2, 4 * D...]
where the time goes in v5:
time: 107 us; the launch traced here: 106 us
  blocking collectives  45.7 us (43%)
  waiting for transfers between devices  26.4 us (25%)
  starting transfers between devices  23.4 us (22%)
  Pallas kernels  8.88 us (8%)
    all_to_all x2, blocking collectives, exchange(): return lax.all_to_all(value, axes, split_axis=0, concat_axis=0, tiled=True)  34.6 us
    all_to_all x2, starting transfers between devices, exchange(): return lax.all_to_all(value, axes, split_axis=0, concat_axis=0, tiled=True)  18.8 us
    all_to_all x2, waiting for transfers between devices, exchange(): return lax.all_to_all(value, axes, split_axis=0, concat_axis=0, tiled=True)  18.5 us
    all_gather x1, blocking collectives, per_device(): other = lax.all_gather(share, 'x', axis=0, tiled=True)  11.1 us
    ppermute x2, waiting for transfers between devices, swap(): return lax.ppermute(value, axis, [(0, 1), (1, 0)])  7.9 us
    ppermute x2, starting transfers between devices, swap(): return lax.ppermute(value, axis, [(0, 1), (1, 0)])  4.67 us
    pallas_call x1, Pallas kernels, spread(): pl.pallas_call(spread_kernel, out_shape=jax.ShapeDtypeStruct((4, 2, 4 * D...  4.55 us
    pallas_call x1, Pallas kernels, products(): pl.pallas_call(products_kernel, out_shape=STACKED, in_specs=[whole()] * l...  2.14 us
  transfers between devices with their start and end apart: 4, of which 4 were waited for; matrix products, arithmetic and copies ran while one was open for 1% of the time, Pallas kernels for 2%

profile of v5, /device:TPU:1, one launch (start us, length us, event | category | flops | bytes accessed | tf_op | source)
XLA Modules:
  0.0 106.0 jit_solution(10547436835711740970)
XLA Ops:
  0.6 10.2 %all-to-all-start = ((bf16[4,4,24,192]{3,2,1,0:T(8,128)(2,1)}), bf16[4,4,24,192]{3,2,1,0:T(8,128)(2,1)S(1)}, u32[]{:S(2)}, u32[]{:S(2)}) async-start(bf16[4,4,24,192]{3,2,1,0:T(8,128)(2,1)} %bitcast.16), calls=%async_computation | async-start | bytes 393216 | tf_op jit(solution)/shard_map/all_to_all | solution.py:203
  10.9 0.9 dynamic-slice_bitcast_fusion
  11.8 7.5 %all-to-all-done.in_ref = bf16[4,4,24,192]{3,2,1,0:T(8,128)(2,1)S(1)} async-done(((bf16[4,4,24,192]{3,2,1,0:T(8,128)(2,1)}), bf16[4,4,24,192]{3,2,1,0:T(8,128)(2,1)S(1)}, u32[]{:S(2)}, u32[]{:S(2)}) %all-to-all-start) | async-done | bytes 147488 | tf_op jit(solution)/shard_map/all_to_all | solution.py:203
  19.2 1.2 %fan.1 = bf16[8,4,24,768]{3,2,1,0:T(8,128)(2,1)} custom-call(bf16[4,4,24,192]{3,2,1,0:T(8,128)(2,1)S(1)} %all-to-all-done.in_ref), custom_call_target="tpu_custom_call" | custom-call | tf_op jit(solution)/shard_map/fan/pallas_call | solution.py:40
  20.4 0.0 copy-start
  20.4 8.6 %all-to-all-start.1 = ((bf16[8,4,24,768]{3,2,1,0:T(8,128)(2,1)}), bf16[8,4,24,768]{3,2,1,0:T(8,128)(2,1)S(1)}, u32[]{:S(2)}, u32[]{:S(2)}) async-start(bf16[8,4,24,768]{3,2,1,0:T(8,128)(2,1)} %fan.1), calls=%async_computation.1 | async-start | bytes 2359296 | tf_op jit(solution)/shard_map/all_to_all | solution.py:203
  29.0 2.3 %collective-permute-start = (bf16[96,768]{1,0:T(8,128)(2,1)S(1)}, bf16[96,768]{1,0:T(8,128)(2,1)S(1)}, u32[]{:S(2)}, u32[]{:S(2)}) collective-permute-start(bf16[96,768]{1,0:T(8,128)(2,1)S(1)} %dynamic-slice_bitcast_fusion), channel_id=1, source_target_pairs={{0,256},{256,0},{1,257},{257,1},{2,258},{258,2},{3,259},{259,3},{4... | collective-permute-start | bytes 442376 | tf_op jit(solution)/shard_map/ppermute | solution.py:199
  31.3 7.6 %collective-permute-done = bf16[96,768]{1,0:T(8,128)(2,1)S(1)} collective-permute-done((bf16[96,768]{1,0:T(8,128)(2,1)S(1)}, bf16[96,768]{1,0:T(8,128)(2,1)S(1)}, u32[]{:S(2)}, u32[]{:S(2)}) %collective-permute-start) | collective-permute-done | bytes 147488 | tf_op jit(solution)/shard_map/ppermute | solution.py:199
  38.9 11.1 %all_gather.3.other_ref = bf16[384,768]{1,0:T(8,128)(2,1)S(1)} all-gather(bf16[96,768]{1,0:T(8,128)(2,1)S(1)} %collective-permute-done), channel_id=1, replica_groups=mesh['y_hi'=2,'z'=8,'core'=2,'y_lo'=4,'x'=4] {'x'}, dimensions={0}, use_global_device_ids=true | all-gather | bytes 737280 | tf_op jit(solution)/shard_map/all_gather | solution.py:212
  50.0 11.0 %all-to-all-done.1 = bf16[8,4,24,768]{3,2,1,0:T(8,128)(2,1)S(1)} async-done(((bf16[8,4,24,768]{3,2,1,0:T(8,128)(2,1)}), bf16[8,4,24,768]{3,2,1,0:T(8,128)(2,1)S(1)}, u32[]{:S(2)}, u32[]{:S(2)}) %all-to-all-start.1) | async-done | bytes 1179680 | tf_op jit(solution)/shard_map/all_to_all | solution.py:203
  61.0 2.4 %collective-permute-start.1 = (bf16[8,4,24,768]{3,2,1,0:T(8,128)(2,1)S(1)}, bf16[8,4,24,768]{3,2,1,0:T(8,128)(2,1)S(1)}, u32[]{:S(2)}, u32[]{:S(2)}) collective-permute-start(bf16[8,4,24,768]{3,2,1,0:T(8,128)(2,1)S(1)} %all-to-all-done.1), channel_id=1, source_target_pairs={{0,16},{16,0},{1,17},{17,1},{2,18},{18,2},{3,19},{19,3},{4,20},{20... | collective-permute-start | bytes 3538952 | tf_op jit(solution)/shard_map/ppermute | solution.py:199
  63.4 0.0 copy-done
  63.4 2.1 %products.1 = (bf16[4,768,192]{2,1,0:T(8,128)(2,1)S(1)}, f32[4,128]{1,0:T(4,128)S(1)}) custom-call(bf16[384,768]{1,0:T(8,128)(2,1)S(1)} %bitcast.13, bf16[384,768]{1,0:T(8,128)(2,1)S(1)} %all_gather.3.other_ref, bf16[8,2,48,768]{3,2,1,0:T(8,128)(2,1)S(1)} %bitcast.10), custom_call_target="tpu_custom_call" | custom-call | tf_op jit(solution)/shard_map/products/pallas_call | solution.py:101
  65.5 0.3 collective-permute-done.1
  65.8 4.6 %spread.1 = bf16[4,2,592,128]{3,2,1,0:T(8,128)(2,1)S(1)} custom-call(bf16[384,768]{1,0:T(8,128)(2,1)S(1)} %bitcast.14, bf16[384,768]{1,0:T(8,128)(2,1)S(1)} %all_gather.3.other_ref, bf16[8,2,48,768]{3,2,1,0:T(8,128)(2,1)S(1)} %bitcast.11, bf16[8,2,48,768]{3,2,1,0:T(8,128)(2,1)S(1)} %bitcast.15, bf16[4,768,192]{2,1,0:T(8,128)(2,1)S(1)} %get-tuple-element.12.stack0_ref, ...), custom_call_target="tpu_custom_call" | custom-call | tf_op jit(solution)/shard_map/spread/pallas_call | solution.py:139
  70.4 20.1 %all_to_all.20.got_ref = bf16[4,2,592,128]{3,2,1,0:T(8,128)(2,1)S(1)} all-to-all(bf16[4,2,592,128]{3,2,1,0:T(8,128)(2,1)S(1)} %spread.1), channel_id=1, replica_groups=mesh['y_hi'=2,'z'=8,'core'=2,'y_lo'=4,'x'=4] {'x'}, dimensions={0} | all-to-all | bytes 2424832 | tf_op jit(solution)/shard_map/all_to_all | solution.py:203
  90.5 0.3 middle.1
  90.7 14.5 %all_to_all.21.got_ref = bf16[8,160,128]{2,1,0:T(8,128)(2,1)S(1)} all-to-all(bf16[8,160,128]{2,1,0:T(8,128)(2,1)S(1)} %middle.1), channel_id=1, replica_groups=mesh['y_hi'=2,'z'=8,'core'=2,'y_lo'=4,'x'=4] {'y_hi','y_lo'}, dimensions={0} | all-to-all | bytes 655360 | tf_op jit(solution)/shard_map/all_to_all | solution.py:203
  105.2 0.7 close.1
Async XLA Ops:
  0.6 18.6 %all-to-all-start = ((bf16[4,4,24,192]{3,2,1,0:T(8,128)(2,1)}), bf16[4,4,24,192]{3,2,1,0:T(8,128)(2,1)S(1)}, u32[]{:S(2)}, u32[]{:S(2)}) async-start(bf16[4,4,24,192]{3,2,1,0:T(8,128)(2,1)} %bitcast.16), calls=%async_computation | async-start | bytes 393216 | tf_op jit(solution)/shard_map/all_to_all | solution.py:203
  20.4 43.0 %copy-start = (bf16[2,768,192]{1,2,0:T(8,128)(2,1)S(1)}, bf16[2,768,192]{1,2,0:T(8,128)(2,1)}, u32[]{:S(2)}) copy-start(bf16[2,768,192]{1,2,0:T(8,128)(2,1)} %param.3) | copy-start | bytes 1769476
  20.4 40.6 %all-to-all-start.1 = ((bf16[8,4,24,768]{3,2,1,0:T(8,128)(2,1)}), bf16[8,4,24,768]{3,2,1,0:T(8,128)(2,1)S(1)}, u32[]{:S(2)}, u32[]{:S(2)}) async-start(bf16[8,4,24,768]{3,2,1,0:T(8,128)(2,1)} %fan.1), calls=%async_computation.1 | async-start | bytes 2359296 | tf_op jit(solution)/shard_map/all_to_all | solution.py:203
  29.0 9.9 %collective-permute-start = (bf16[96,768]{1,0:T(8,128)(2,1)S(1)}, bf16[96,768]{1,0:T(8,128)(2,1)S(1)}, u32[]{:S(2)}, u32[]{:S(2)}) collective-permute-start(bf16[96,768]{1,0:T(8,128)(2,1)S(1)} %dynamic-slice_bitcast_fusion), channel_id=1, source_target_pairs={{0,256},{256,0},{1,257},{257,1},{2,258},{258,2},{3,259},{259,3},{4... | collective-permute-start | bytes 442376 | tf_op jit(solution)/shard_map/ppermute | solution.py:199
  61.0 4.9 %collective-permute-start.1 = (bf16[8,4,24,768]{3,2,1,0:T(8,128)(2,1)S(1)}, bf16[8,4,24,768]{3,2,1,0:T(8,128)(2,1)S(1)}, u32[]{:S(2)}, u32[]{:S(2)}) collective-permute-start(bf16[8,4,24,768]{3,2,1,0:T(8,128)(2,1)S(1)} %all-to-all-done.1), channel_id=1, source_target_pairs={{0,16},{16,0},{1,17},{17,1},{2,18},{18,2},{3,19},{19,3},{4,20},{20... | collective-permute-start | bytes 3538952 | tf_op jit(solution)/shard_map/ppermute | solution.py:199

commit v6 on v5

--- a/solution.py
+++ b/solution.py
@@ -207,7 +207,6 @@
     turned = jnp.swapaxes(green, 1, 2).reshape(WPER * NOCC, M)
     share = lax.dynamic_index_in_dim(turned.reshape(4, SHARE, M), lax.axis_index("x"), 0, keepdims=False)
     packed = exchange(chol_vectors.reshape(4, QUARTER, ROWS, NOCC), ("y_hi", "core"))
-    packed, share = lax.optimization_barrier((packed, share))
     share = swap(share, "y_hi")
     other = lax.all_gather(share, "x", axis=0, tiled=True)
     own = exchange(fan(packed), "z")

time: 107 us -> 108 us (level)
  blocking collectives: 45.7 us -> 65 us
  starting transfers between devices: 23.4 us -> 12.9 us
  waiting for transfers between devices: 26.4 us -> 18.5 us
    all_to_all x2 -> x3, blocking collectives: 34.6 us -> 53.2 us  [exchange(): return lax.all_to_all(value, axes, split_axis=0, concat_axis=0, tiled=True)]
    all_to_all x2 -> x1, starting transfers between devices: 18.8 us -> 8.56 us  [exchange(): return lax.all_to_all(value, axes, split_axis=0, concat_axis=0, tiled=True)]
    all_to_all x2 -> x1, waiting for transfers between devices: 18.5 us -> 10 us  [exchange(): return lax.all_to_all(value, axes, split_axis=0, concat_axis=0, tiled=True)]
  transfers between devices with their start and end apart: 4 -> 3, of which waited for: 4 -> 3; matrix products, arithmetic and copies ran while one was open for 1% -> 0% of each run, Pallas kernels for 2% -> 2%
where the time goes in v6:
time: 108 us; the launch traced here: 106 us
  blocking collectives  65 us (60%)
  waiting for transfers between devices  18.5 us (17%)
  starting transfers between devices  12.9 us (12%)
  Pallas kernels  8.9 us (8%)
    all_to_all x3, blocking collectives, exchange(): return lax.all_to_all(value, axes, split_axis=0, concat_axis=0, tiled=True)  53.2 us
    all_gather x1, blocking collectives, per_device(): other = lax.all_gather(share, 'x', axis=0, tiled=True)  11.8 us
    all_to_all x1, waiting for transfers between devices, exchange(): return lax.all_to_all(value, axes, split_axis=0, concat_axis=0, tiled=True)  10 us
    all_to_all x1, starting transfers between devices, exchange(): return lax.all_to_all(value, axes, split_axis=0, concat_axis=0, tiled=True)  8.56 us
    ppermute x2, waiting for transfers between devices, swap(): return lax.ppermute(value, axis, [(0, 1), (1, 0)])  8.53 us
    pallas_call x1, Pallas kernels, spread(): pl.pallas_call(spread_kernel, out_shape=jax.ShapeDtypeStruct((4, 2, 4 * D...  4.58 us
    ppermute x2, starting transfers between devices, swap(): return lax.ppermute(value, axis, [(0, 1), (1, 0)])  4.36 us
  transfers between devices with their start and end apart: 3, of which 3 were waited for; matrix products, arithmetic and copies ran while one was open for 0% of the time, Pallas kernels for 2%

profile of v6, /device:TPU:1, one launch (start us, length us, event | category | flops | bytes accessed | tf_op | source)
XLA Modules:
  0.0 106.1 jit_solution(17135739265898201811)
XLA Ops:
  0.6 18.7 %all_to_all.20.in_ref = bf16[4,4,24,192]{3,2,1,0:T(8,128)(2,1)S(1)} all-to-all(bf16[4,4,24,192]{3,2,1,0:T(8,128)(2,1)} %bitcast.16), channel_id=1, replica_groups=mesh['y_hi'=2,'z'=8,'core'=2,'y_lo'=4,'x'=4] {'y_hi','core'}, dimensions={0} | all-to-all | bytes 294912 | tf_op jit(solution)/shard_map/all_to_all | solution.py:203
  19.3 1.2 %fan.1 = bf16[8,4,24,768]{3,2,1,0:T(8,128)(2,1)} custom-call(bf16[4,4,24,192]{3,2,1,0:T(8,128)(2,1)S(1)} %all_to_all.20.in_ref), custom_call_target="tpu_custom_call" | custom-call | tf_op jit(solution)/shard_map/fan/pallas_call | solution.py:40
  20.5 0.0 copy-start
  20.5 8.6 %all-to-all-start.1 = ((bf16[8,4,24,768]{3,2,1,0:T(8,128)(2,1)}), bf16[8,4,24,768]{3,2,1,0:T(8,128)(2,1)S(1)}, u32[]{:S(2)}, u32[]{:S(2)}) async-start(bf16[8,4,24,768]{3,2,1,0:T(8,128)(2,1)} %fan.1), calls=%async_computation.1 | async-start | bytes 2359296 | tf_op jit(solution)/shard_map/all_to_all | solution.py:203
  29.1 0.0 copy-done
  29.1 2.0 %collective-permute-start = (bf16[96,768]{1,0:T(8,128)(2,1)S(1)}, bf16[96,768]{1,0:T(8,128)(2,1)S(1)}, u32[]{:S(2)}, u32[]{:S(2)}) collective-permute-start(bf16[96,768]{1,0:T(8,128)(2,1)S(1)} %dynamic-slice_bitcast_fusion), channel_id=1, source_target_pairs={{0,256},{256,0},{1,257},{257,1},{2,258},{258,2},{3,259},{259,3},{4... | collective-permute-start | bytes 442376 | tf_op jit(solution)/shard_map/ppermute | solution.py:199
  31.1 8.2 %collective-permute-done = bf16[96,768]{1,0:T(8,128)(2,1)S(1)} collective-permute-done((bf16[96,768]{1,0:T(8,128)(2,1)S(1)}, bf16[96,768]{1,0:T(8,128)(2,1)S(1)}, u32[]{:S(2)}, u32[]{:S(2)}) %collective-permute-start) | collective-permute-done | bytes 147488 | tf_op jit(solution)/shard_map/ppermute | solution.py:199
  39.3 11.8 %all_gather.3.other_ref = bf16[384,768]{1,0:T(8,128)(2,1)S(1)} all-gather(bf16[96,768]{1,0:T(8,128)(2,1)S(1)} %collective-permute-done), channel_id=1, replica_groups=mesh['y_hi'=2,'z'=8,'core'=2,'y_lo'=4,'x'=4] {'x'}, dimensions={0}, use_global_device_ids=true | all-gather | bytes 737280 | tf_op jit(solution)/shard_map/all_gather | solution.py:211
  51.1 10.0 %all-to-all-done.1 = bf16[8,4,24,768]{3,2,1,0:T(8,128)(2,1)S(1)} async-done(((bf16[8,4,24,768]{3,2,1,0:T(8,128)(2,1)}), bf16[8,4,24,768]{3,2,1,0:T(8,128)(2,1)S(1)}, u32[]{:S(2)}, u32[]{:S(2)}) %all-to-all-start.1) | async-done | bytes 1179680 | tf_op jit(solution)/shard_map/all_to_all | solution.py:203
  61.1 2.4 %collective-permute-start.1 = (bf16[8,4,24,768]{3,2,1,0:T(8,128)(2,1)S(1)}, bf16[8,4,24,768]{3,2,1,0:T(8,128)(2,1)S(1)}, u32[]{:S(2)}, u32[]{:S(2)}) collective-permute-start(bf16[8,4,24,768]{3,2,1,0:T(8,128)(2,1)S(1)} %all-to-all-done.1), channel_id=1, source_target_pairs={{0,16},{16,0},{1,17},{17,1},{2,18},{18,2},{3,19},{19,3},{4,20},{20... | collective-permute-start | bytes 3538952 | tf_op jit(solution)/shard_map/ppermute | solution.py:199
  63.5 2.1 %products.1 = (bf16[4,768,192]{2,1,0:T(8,128)(2,1)S(1)}, f32[4,128]{1,0:T(4,128)S(1)}) custom-call(bf16[384,768]{1,0:T(8,128)(2,1)S(1)} %bitcast.13, bf16[384,768]{1,0:T(8,128)(2,1)S(1)} %all_gather.3.other_ref, bf16[8,2,48,768]{3,2,1,0:T(8,128)(2,1)S(1)} %bitcast.10), custom_call_target="tpu_custom_call" | custom-call | tf_op jit(solution)/shard_map/products/pallas_call | solution.py:101
  65.7 0.3 collective-permute-done.1
  66.0 4.6 %spread.1 = bf16[4,2,592,128]{3,2,1,0:T(8,128)(2,1)S(1)} custom-call(bf16[384,768]{1,0:T(8,128)(2,1)S(1)} %bitcast.14, bf16[384,768]{1,0:T(8,128)(2,1)S(1)} %all_gather.3.other_ref, bf16[8,2,48,768]{3,2,1,0:T(8,128)(2,1)S(1)} %bitcast.11, bf16[8,2,48,768]{3,2,1,0:T(8,128)(2,1)S(1)} %bitcast.15, bf16[4,768,192]{2,1,0:T(8,128)(2,1)S(1)} %get-tuple-element.8.stack0_ref, ...), custom_call_target="tpu_custom_call" | custom-call | tf_op jit(solution)/shard_map/spread/pallas_call | solution.py:139
  70.6 20.1 %all_to_all.21.got_ref = bf16[4,2,592,128]{3,2,1,0:T(8,128)(2,1)S(1)} all-to-all(bf16[4,2,592,128]{3,2,1,0:T(8,128)(2,1)S(1)} %spread.1), channel_id=1, replica_groups=mesh['y_hi'=2,'z'=8,'core'=2,'y_lo'=4,'x'=4] {'x'}, dimensions={0} | all-to-all | bytes 2424832 | tf_op jit(solution)/shard_map/all_to_all | solution.py:203
  90.7 0.3 middle.1
  90.9 14.4 %all_to_all.22.got_ref = bf16[8,160,128]{2,1,0:T(8,128)(2,1)S(1)} all-to-all(bf16[8,160,128]{2,1,0:T(8,128)(2,1)S(1)} %middle.1), channel_id=1, replica_groups=mesh['y_hi'=2,'z'=8,'core'=2,'y_lo'=4,'x'=4] {'y_hi','y_lo'}, dimensions={0} | all-to-all | bytes 655360 | tf_op jit(solution)/shard_map/all_to_all | solution.py:203
  105.4 0.7 close.1
  (1 shorter events, 0.0 us)
Async XLA Ops:
  20.5 8.6 %copy-start = (bf16[2,768,192]{1,2,0:T(8,128)(2,1)S(1)}, bf16[2,768,192]{1,2,0:T(8,128)(2,1)}, u32[]{:S(2)}) copy-start(bf16[2,768,192]{1,2,0:T(8,128)(2,1)} %param.3) | copy-start | bytes 1769476
  20.5 40.6 %all-to-all-start.1 = ((bf16[8,4,24,768]{3,2,1,0:T(8,128)(2,1)}), bf16[8,4,24,768]{3,2,1,0:T(8,128)(2,1)S(1)}, u32[]{:S(2)}, u32[]{:S(2)}) async-start(bf16[8,4,24,768]{3,2,1,0:T(8,128)(2,1)} %fan.1), calls=%async_computation.1 | async-start | bytes 2359296 | tf_op jit(solution)/shard_map/all_to_all | solution.py:203
  29.1 10.2 %collective-permute-start = (bf16[96,768]{1,0:T(8,128)(2,1)S(1)}, bf16[96,768]{1,0:T(8,128)(2,1)S(1)}, u32[]{:S(2)}, u32[]{:S(2)}) collective-permute-start(bf16[96,768]{1,0:T(8,128)(2,1)S(1)} %dynamic-slice_bitcast_fusion), channel_id=1, source_target_pairs={{0,256},{256,0},{1,257},{257,1},{2,258},{258,2},{3,259},{259,3},{4... | collective-permute-start | bytes 442376 | tf_op jit(solution)/shard_map/ppermute | solution.py:199
  61.1 4.8 %collective-permute-start.1 = (bf16[8,4,24,768]{3,2,1,0:T(8,128)(2,1)S(1)}, bf16[8,4,24,768]{3,2,1,0:T(8,128)(2,1)S(1)}, u32[]{:S(2)}, u32[]{:S(2)}) collective-permute-start(bf16[8,4,24,768]{3,2,1,0:T(8,128)(2,1)S(1)} %all-to-all-done.1), channel_id=1, source_target_pairs={{0,16},{16,0},{1,17},{17,1},{2,18},{18,2},{3,19},{19,3},{4,20},{20... | collective-permute-start | bytes 3538952 | tf_op jit(solution)/shard_map/ppermute | solution.py:199
